TPU v7x, 512 devices: a whole 4x8x8 slice. The times are simulated.
512 devices in a mesh: dp: 32 (over z, x), seq: 16 (over y, core).
Axes of the slice: x: 4, y: 8, z: 8, core: 2. Of those that a mesh axis runs over, the one named last changes fastest.
Arguments:
- hidden: bfloat16 [65536, 4096], P(('dp', 'seq')), may hold values from -6 to 6
- frozen_query: bfloat16 [65536, 2048], P(('dp', 'seq')), may hold values from -6 to 6
- frozen_key: bfloat16 [65536, 512], P(('dp', 'seq')), may hold values from -6 to 6
- frozen_value: bfloat16 [65536, 512], P(('dp', 'seq')), may hold values from -6 to 6
- upstream: bfloat16 [65536, 2048], P(('dp', 'seq')), may hold values from -0.078125 to 0.078125
- destination_group: int32 [65536], P(('dp', 'seq')), may hold values from 0 to 31, as said below
- destination_slot: int32 [65536], P(('dp', 'seq')), may hold values from 0 to 127, as said below
- segment_labels: int32 [32, 2048], P('dp', 'seq'), may hold values from 0 to 3, never falling along the last dimension, each value on 1 to 1024 neighbouring positions
- adapter_down_weight: bfloat16 [16, 4096], replicated, may hold values from -0.09375 to 0.09375
- adapter_up_weight: bfloat16 [16, 512], replicated, may hold values from -0.75 to 0.75
Outputs:
- attended: bfloat16 [65536, 2048], P(('dp', 'seq'))
- grad_down: float32 [16, 4096], replicated
- up_gradient: float32 [16, 512], replicated
Inputs may be any that keep to these rules, and one draw needn't show every extreme that they name: `destination_group`: the rows of the loader device at index d along dp and s along seq go to devices of their groups with the same index s along seq. No loader device sends more than 8 rows to one group, and each sends exactly 8 to some group. `destination_slot`: each device of a group receives rows at every position 0 to 127 exactly once.
All inputs are finite; a program needn't handle non-finite values.
Results may differ from a plain program's by a relative error of at most 0.007.
Values may be sent and summed in bfloat16 or wider, within the bound.
A program may use at most 64 MiB of HBM per device.

v0:
```python
import math

import jax
import jax.numpy as jnp
from jax import lax
from jax.sharding import PartitionSpec as P

HEAD_SIZE = 128


adapter_scale = 2.0


def contract_over_rows(left, right):
    return lax.dot_general(
        left, right, (((0,), (0,)), ((), ())), preferred_element_type=jnp.float32
    )


def narrow_rank_value(row_entries, adapter_down_weight):
    return lax.dot_general(
        row_entries,
        adapter_down_weight,
        (((1,), (1,)), ((), ())),
        preferred_element_type=jnp.float32,
    ).astype(jnp.bfloat16)


def adapted_value(plain_value, reduced_total, adapter_up_weight):
    return (
        plain_value.astype(jnp.float32)
        + adapter_scale
        * jnp.dot(reduced_total, adapter_up_weight, preferred_element_type=jnp.float32)
    ).astype(jnp.bfloat16)


def settle(row_entries, destination, row_count):
    return (
        jnp.zeros((row_count,) + row_entries.shape[1:], row_entries.dtype)
        .at[destination]
        .set(row_entries, mode="drop")
    )


def attend(items):
    queries = items[0][:, 0]
    key_heads = items[1][:, 0]
    value_heads = items[2][:, 0]
    grad_heads = items[3][:, 0]
    labels = items[4][:, 0]
    length, head_count, head_width = queries.shape
    block_rows = min(512, length)
    segments = labels[:, 0]
    positions = jnp.arange(length, dtype=jnp.int32)
    score_scale = 1.0 / math.sqrt(head_width)

    def block_step(carry, block_index):
        row_start = block_index * block_rows
        query_block = lax.dynamic_slice_in_dim(queries, row_start, block_rows, 0)
        grad_block = lax.dynamic_slice_in_dim(grad_heads, row_start, block_rows, 0)
        label_block = lax.dynamic_slice_in_dim(segments, row_start, block_rows, 0)
        place_block = lax.dynamic_slice_in_dim(positions, row_start, block_rows, 0)
        scores = (
            jnp.einsum("qhd,khd->hqk", query_block, key_heads, preferred_element_type=jnp.float32)
            * score_scale
        )
        allowed = (positions[None, :] <= place_block[:, None]) & (
            segments[None, :] == label_block[:, None]
        )
        scores = jnp.where(allowed[None], scores, -jnp.inf)
        row_max = jnp.max(scores, axis=2, keepdims=True)
        exponent = jnp.exp(scores - row_max)
        attn_weights = (exponent / jnp.sum(exponent, axis=2, keepdims=True)).astype(jnp.bfloat16)
        attended = jnp.einsum(
            "hqk,khd->qhd", attn_weights, value_heads, preferred_element_type=jnp.float32
        )
        carry = carry + jnp.einsum(
            "hqk,qhd->khd", attn_weights, grad_block, preferred_element_type=jnp.float32
        )
        return (carry, attended.astype(jnp.bfloat16))

    start_grads = jnp.zeros((length, head_count, head_width), jnp.float32)
    value_grad, attended = lax.scan(
        block_step, start_grads, jnp.arange(length // block_rows, dtype=jnp.int32)
    )
    attended = attended.reshape(length, head_count, head_width)
    return (attended[:, None], value_grad.astype(jnp.bfloat16)[:, None])


def shards(
    hidden,
    frozen_query,
    frozen_key,
    frozen_value,
    upstream,
    destination_group,
    destination_slot,
    segment_labels,
    adapter_down_weight,
    adapter_up_weight,
):
    groups = lax.axis_size("dp")
    seq_count = lax.axis_size("seq")
    row_count = hidden.shape[0]
    capacity = 2 * row_count // groups
    slot_total = groups * capacity
    onehot = (destination_group[:, None] == jnp.arange(groups, dtype=jnp.int32)[None, :]).astype(
        jnp.int32
    )
    running = jnp.cumsum(onehot, axis=0) - 1
    send_place = destination_group * capacity + jnp.sum(running * onehot, axis=1)

    def pack(row_entries):
        return (
            jnp.zeros((slot_total,) + row_entries.shape[1:], row_entries.dtype)
            .at[send_place]
            .set(row_entries)
        )

    send_label = jnp.full((slot_total,), -1, jnp.int32).at[send_place].set(destination_slot)
    arrived_data = (
        lax.all_to_all(pack(hidden), "dp", split_axis=0, concat_axis=0, tiled=True),
        lax.all_to_all(pack(frozen_query), "dp", split_axis=0, concat_axis=0, tiled=True),
        lax.all_to_all(pack(frozen_key), "dp", split_axis=0, concat_axis=0, tiled=True),
        lax.all_to_all(pack(frozen_value), "dp", split_axis=0, concat_axis=0, tiled=True),
        lax.all_to_all(pack(upstream), "dp", split_axis=0, concat_axis=0, tiled=True),
        lax.all_to_all(send_label, "dp", split_axis=0, concat_axis=0, tiled=True),
    )
    arrived = arrived_data[5]
    destination = jnp.where(arrived >= 0, arrived, row_count)
    local_hidden = settle(arrived_data[0], destination, row_count)
    query_rows = settle(arrived_data[1], destination, row_count)
    key_rows = settle(arrived_data[2], destination, row_count)
    plain_value = settle(arrived_data[3], destination, row_count)
    grad_rows = settle(arrived_data[4], destination, row_count)
    local_reduced = narrow_rank_value(local_hidden, adapter_down_weight)
    local_value = adapted_value(plain_value, local_reduced, adapter_up_weight)
    head_count = query_rows.shape[1] // HEAD_SIZE
    kv_count = key_rows.shape[1] // HEAD_SIZE
    group_ratio = head_count // kv_count
    per_device = head_count // seq_count
    query_heads = query_rows.reshape(row_count, seq_count, per_device, HEAD_SIZE)
    key_heads = jnp.repeat(
        key_rows.reshape(row_count, kv_count, HEAD_SIZE), group_ratio, axis=1
    ).reshape(row_count, seq_count, per_device, HEAD_SIZE)
    value_heads = jnp.repeat(
        local_value.reshape(row_count, kv_count, HEAD_SIZE), group_ratio, axis=1
    ).reshape(row_count, seq_count, per_device, HEAD_SIZE)
    grad_heads = grad_rows.reshape(row_count, seq_count, per_device, HEAD_SIZE)
    labels = jnp.broadcast_to(
        segment_labels.reshape(row_count, 1, 1), (row_count, seq_count, per_device)
    )
    attended_heads, head_grads = attend(
        (
            lax.all_to_all(query_heads, "seq", split_axis=1, concat_axis=0, tiled=True),
            lax.all_to_all(key_heads, "seq", split_axis=1, concat_axis=0, tiled=True),
            lax.all_to_all(value_heads, "seq", split_axis=1, concat_axis=0, tiled=True),
            lax.all_to_all(grad_heads, "seq", split_axis=1, concat_axis=0, tiled=True),
            lax.all_to_all(labels, "seq", split_axis=1, concat_axis=0, tiled=True),
        )
    )
    returned = (
        lax.all_to_all(attended_heads, "seq", split_axis=0, concat_axis=1, tiled=True),
        lax.all_to_all(head_grads, "seq", split_axis=0, concat_axis=1, tiled=True),
    )
    attended = returned[0].reshape(row_count, head_count * HEAD_SIZE)
    value_gradients = (
        returned[1].astype(jnp.float32).reshape(row_count, kv_count, group_ratio, HEAD_SIZE)
    )
    value_gradients = (
        jnp.sum(value_gradients, axis=2)
        .astype(jnp.bfloat16)
        .reshape(row_count, kv_count * HEAD_SIZE)
    )
    reduced_gradient = (
        adapter_scale
        * lax.dot_general(
            value_gradients,
            adapter_up_weight,
            (((1,), (1,)), ((), ())),
            preferred_element_type=jnp.float32,
        )
    ).astype(jnp.bfloat16)
    up_gradient_part = adapter_scale * contract_over_rows(local_reduced, value_gradients)
    grad_down_part = contract_over_rows(reduced_gradient, local_hidden)
    totals = lax.psum((grad_down_part, up_gradient_part), ("dp", "seq"))
    return (attended, totals[0], totals[1])


def solution(mesh):
    return jax.shard_map(
        shards,
        mesh=mesh,
        in_specs=(
            P(("dp", "seq"), None),
            P(("dp", "seq"), None),
            P(("dp", "seq"), None),
            P(("dp", "seq"), None),
            P(("dp", "seq"), None),
            P(("dp", "seq")),
            P(("dp", "seq")),
            P("dp", "seq"),
            P(),
            P(),
        ),
        out_specs=(P(("dp", "seq"), None), P(), P()),
        check_vma=False,
    )
```

profile of v0, /device:TPU:1, one launch (start us, length us, event | category | flops | bytes accessed | tf_op | source)
XLA Modules:
  0.0 633.3 jit_solution(12370632439482228371)
XLA Ops:
  10.8 22.1 %all_to_all.174 = s32[32,8,1]{1,2,0:T(1,128)S(1)} all-to-all(s32[32,8,1]{1,2,0:T(1,128)S(1)} %bitcast.158), channel_id=1, replica_groups=mesh['dp'=32,'seq'=16] {'dp'}, dimensions={0} | all-to-all | bytes 2048 | tf_op jit(solution)/shard_map/all_to_all | solution.py:127
  34.2 9.2 %all-to-all-start.3 = ((s32[128,16,1]{0,2,1:T(1,128)}), s32[128,16,1]{0,2,1:T(1,128)S(1)}, u32[]{:S(2)}, u32[]{:S(2)}) async-start(s32[128,16,1]{0,2,1:T(1,128)} %broadcast_in_dim.70), calls=%async_computation.3 | async-start | bytes 16384 | tf_op jit(solution)/shard_map/all_to_all | solution.py:159
  43.4 2.1 scatter_custom_fusion.5
  45.5 4.8 all-to-all-done.3
  50.3 3.9 all-to-all-start.6
  54.2 2.1 scatter_custom_fusion.7
  56.3 9.4 %all-to-all-done.6 = bf16[32,8,512]{2,1,0:T(8,128)(2,1)S(1)} async-done(((bf16[32,8,512]{2,1,0:T(8,128)(2,1)}), bf16[32,8,512]{2,1,0:T(8,128)(2,1)S(1)}, u32[]{:S(2)}, u32[]{:S(2)}) %all-to-all-start.6) | async-done | bytes 262176 | tf_op jit(solution)/shard_map/all_to_all | solution.py:124
  65.7 4.5 all-to-all-start.8
  73.1 7.5 %all-to-all-done.8 = bf16[32,8,512]{2,1,0:T(8,128)(2,1)S(1)} async-done(((bf16[32,8,512]{2,1,0:T(8,128)(2,1)}), bf16[32,8,512]{2,1,0:T(8,128)(2,1)S(1)}, u32[]{:S(2)}, u32[]{:S(2)}) %all-to-all-start.8) | async-done | bytes 262176 | tf_op jit(solution)/shard_map/all_to_all | solution.py:125
  81.6 7.1 %all-to-all-start.7 = ((bf16[128,16,1,128]{3,0,2,1:T(8,128)(2,1)}), bf16[128,16,1,128]{3,0,2,1:T(8,128)(2,1)S(1)}, u32[]{:S(2)}, u32[]{:S(2)}) async-start(bf16[128,16,1,128]{3,0,2,1:T(8,128)(2,1)} %bitcast.24), calls=%async_computation.7 | async-start | bytes 1048576 | tf_op jit(solution)/shard_map/all_to_all | solution.py:156
  88.7 3.0 scatter_custom_fusion.3
  91.7 14.4 %all-to-all-done.7 = bf16[128,16,1,128]{3,0,2,1:T(8,128)(2,1)S(1)} async-done(((bf16[128,16,1,128]{3,0,2,1:T(8,128)(2,1)}), bf16[128,16,1,128]{3,0,2,1:T(8,128)(2,1)S(1)}, u32[]{:S(2)}, u32[]{:S(2)}) %all-to-all-start.7) | async-done | bytes 524320 | tf_op jit(solution)/shard_map/all_to_all | solution.py:156
  106.1 3.9 all-to-all-start.4
  110.0 3.0 scatter_custom_fusion.1
  113.0 24.2 %all-to-all-done.4 = bf16[32,8,2048]{2,1,0:T(8,128)(2,1)S(1)} async-done(((bf16[32,8,2048]{2,1,0:T(8,128)(2,1)}), bf16[32,8,2048]{2,1,0:T(8,128)(2,1)S(1)}, u32[]{:S(2)}, u32[]{:S(2)}) %all-to-all-start.4) | async-done | bytes 1048608 | tf_op jit(solution)/shard_map/all_to_all | solution.py:123
  137.2 5.6 all-to-all-start.1
  142.8 2.2 scatter_custom_fusion.4
  146.0 24.1 %all-to-all-done.1 = bf16[32,8,2048]{2,1,0:T(8,128)(2,1)S(1)} async-done(((bf16[32,8,2048]{2,1,0:T(8,128)(2,1)}), bf16[32,8,2048]{2,1,0:T(8,128)(2,1)S(1)}, u32[]{:S(2)}, u32[]{:S(2)}) %all-to-all-start.1) | async-done | bytes 1048608 | tf_op jit(solution)/shard_map/all_to_all | solution.py:126
  170.1 5.1 all-to-all-start.5
  175.2 4.3 scatter_custom_fusion.9
  179.5 13.0 %all-to-all-done.5 = bf16[128,16,1,128]{0,3,2,1:T(8,128)(2,1)S(1)} async-done(((bf16[128,16,1,128]{0,3,2,1:T(8,128)(2,1)}), bf16[128,16,1,128]{0,3,2,1:T(8,128)(2,1)S(1)}, u32[]{:S(2)}, u32[]{:S(2)}) %all-to-all-start.5) | async-done | bytes 524320 | tf_op jit(solution)/shard_map/all_to_all | solution.py:155
  193.3 5.3 all-to-all-start.9
  198.6 2.8 scatter_custom_fusion.2
  201.5 2.0 copy.43
  203.5 45.8 %all-to-all-done.9 = bf16[32,8,4096]{2,1,0:T(8,128)(2,1)S(1)} async-done(((bf16[32,8,4096]{2,1,0:T(8,128)(2,1)}), bf16[32,8,4096]{2,1,0:T(8,128)(2,1)S(1)}, u32[]{:S(2)}, u32[]{:S(2)}) %all-to-all-start.9) | async-done | bytes 2097184 | tf_op jit(solution)/shard_map/all_to_all | solution.py:122
  249.3 4.1 all-to-all-start.2
  253.5 2.1 scatter_custom_fusion.8
  255.6 3.6 scatter_custom_fusion.10
  259.9 9.9 %all-to-all-done.2 = bf16[128,16,1,128]{0,3,2,1:T(8,128)(2,1)} async-done(((bf16[128,16,1,128]{0,3,2,1:T(8,128)(2,1)}), bf16[128,16,1,128]{0,3,2,1:T(8,128)(2,1)}, u32[]{:S(2)}, u32[]{:S(2)}) %all-to-all-start.2) | async-done | bytes 524320 | tf_op jit(solution)/shard_map/all_to_all | solution.py:158
  270.6 4.3 all-to-all-start.10
  276.0 2.1 copy.45
  278.1 11.6 %all-to-all-done.10 = bf16[128,16,1,128]{3,0,2,1:T(8,128)(2,1)} async-done(((bf16[128,16,1,128]{3,0,2,1:T(8,128)(2,1)}), bf16[128,16,1,128]{3,0,2,1:T(8,128)(2,1)}, u32[]{:S(2)}, u32[]{:S(2)}) %all-to-all-start.10) | async-done | bytes 524320 | tf_op jit(solution)/shard_map/all_to_all | solution.py:157
  289.8 36.0 %while.14 = (s32[]{:T(128)}, f32[2048,1,128]{0,2,1:T(8,128)S(1)}, bf16[4,512,1,128]{3,1,2,0:T(8,128)(2,1)}, s32[4]{0:T(128)S(1)}, bf16[2048,1,128]{2,0,1:T(8,128...) while((s32[]{:T(128)}, f32[2048,1,128]{0,2,1:T(8,128)S(1)}, ...), condition=%wide.region_16.17_spmd.clone.clone, body=%wide.region_13.16_spmd.clone.clone.sunk | while | flops 817429504 | bytes 22452960 | solution.py:83
  291.2 2.2 fusion.72
  296.3 2.4 fusion.75
  300.2 2.3 fusion.72
  305.4 2.4 fusion.75
  309.2 2.2 fusion.72
  314.4 2.4 fusion.75
  318.2 2.3 fusion.72
  323.4 2.4 fusion.75
  328.6 4.2 all-to-all-start.12
  332.7 2.1 reduce.9
  335.7 14.3 %all-to-all-done.12 = bf16[16,2,8192]{2,1,0:T(2,128)(2,1)S(1)} async-done(((bf16[16,2,8192]{2,1,0:T(2,128)(2,1)}), bf16[16,2,8192]{2,1,0:T(2,128)(2,1)S(1)}, u32[]{:S(2)}, u32[]{:S(2)}) %all-to-all-start.12) | async-done | bytes 524320 | tf_op jit(solution)/shard_map/all_to_all | solution.py:164
  350.0 3.5 all-to-all-start.11
  355.8 14.4 %all-to-all-done.11 = bf16[16,2,8192]{2,1,0:T(2,128)(2,1)S(1)} async-done(((bf16[16,2,8192]{2,1,0:T(2,128)(2,1)}), bf16[16,2,8192]{2,1,0:T(2,128)(2,1)S(1)}, u32[]{:S(2)}, u32[]{:S(2)}) %all-to-all-start.11) | async-done | bytes 524320 | tf_op jit(solution)/shard_map/all_to_all | solution.py:163
  372.3 96.7 %psum.15 = f32[16,512]{1,0:T(8,128)} all-reduce(f32[16,512]{1,0:T(8,128)S(1)} %convolution_multiply_fusion.1), channel_id=1, replica_groups=mesh['dp'=32,'seq'=16] {'dp','seq'}, use_global_device_ids=true, to_apply=%region_19.20 | all-reduce | flops 8192 | bytes 65536 | tf_op jit(solution)/shard_map/psum | solution.py:186
  468.9 155.9 %all-reduce.2.cloned.1.call-done = f32[16,4096]{1,0:T(8,128)} async-done(((f32[16,4096]{1,0:T(8,128)}), f32[16,4096]{1,0:T(8,128)}) %all-reduce.2.cloned.1.call-update) | async-done | bytes 262160 | tf_op jit(solution)/shard_map/psum | solution.py:186
  (82 shorter events, 37.3 us)
Async XLA Ops:
  7.2 252.0 %copy-start = (bf16[16,4096]{1,0:T(8,128)(2,1)S(1)}, bf16[16,4096]{1,0:T(8,128)(2,1)}, u32[]{:S(2)}) copy-start(bf16[16,4096]{1,0:T(8,128)(2,1)} %param.20) | copy-start | bytes 393220
  34.2 16.2 %all-to-all-start.3 = ((s32[128,16,1]{0,2,1:T(1,128)}), s32[128,16,1]{0,2,1:T(1,128)S(1)}, u32[]{:S(2)}, u32[]{:S(2)}) async-start(s32[128,16,1]{0,2,1:T(1,128)} %broadcast_in_dim.70), calls=%async_computation.3 | async-start | bytes 16384 | tf_op jit(solution)/shard_map/all_to_all | solution.py:159
  50.3 15.4 %all-to-all-start.6 = ((bf16[32,8,512]{2,1,0:T(8,128)(2,1)}), bf16[32,8,512]{2,1,0:T(8,128)(2,1)S(1)}, u32[]{:S(2)}, u32[]{:S(2)}) async-start(bf16[32,8,512]{2,1,0:T(8,128)(2,1)} %bitcast.22), calls=%async_computation.6 | async-start | bytes 524288 | tf_op jit(solution)/shard_map/all_to_all | solution.py:124
  65.7 14.9 %all-to-all-start.8 = ((bf16[32,8,512]{2,1,0:T(8,128)(2,1)}), bf16[32,8,512]{2,1,0:T(8,128)(2,1)S(1)}, u32[]{:S(2)}, u32[]{:S(2)}) async-start(bf16[32,8,512]{2,1,0:T(8,128)(2,1)} %bitcast.28), calls=%async_computation.8 | async-start | bytes 524288 | tf_op jit(solution)/shard_map/all_to_all | solution.py:125
  81.6 24.5 %all-to-all-start.7 = ((bf16[128,16,1,128]{3,0,2,1:T(8,128)(2,1)}), bf16[128,16,1,128]{3,0,2,1:T(8,128)(2,1)S(1)}, u32[]{:S(2)}, u32[]{:S(2)}) async-start(bf16[128,16,1,128]{3,0,2,1:T(8,128)(2,1)} %bitcast.24), calls=%async_computation.7 | async-start | bytes 1048576 | tf_op jit(solution)/shard_map/all_to_all | solution.py:156
  106.0 31.1 %copy-start.5 = (bf16[128,16,1,128]{3,0,2,1:T(8,128)(2,1)}, bf16[128,16,1,128]{3,0,2,1:T(8,128)(2,1)S(1)}, u32[]{:S(2)}) copy-start(bf16[128,16,1,128]{3,0,2,1:T(8,128)(2,1)S(1)} %all-to-all-done.7) | copy-start | bytes 1572868
  106.1 31.1 %all-to-all-start.4 = ((bf16[32,8,2048]{2,1,0:T(8,128)(2,1)}), bf16[32,8,2048]{2,1,0:T(8,128)(2,1)S(1)}, u32[]{:S(2)}, u32[]{:S(2)}) async-start(bf16[32,8,2048]{2,1,0:T(8,128)(2,1)} %bitcast.15), calls=%async_computation.4 | async-start | bytes 2097152 | tf_op jit(solution)/shard_map/all_to_all | solution.py:123
  137.2 32.9 %all-to-all-start.1 = ((bf16[32,8,2048]{2,1,0:T(8,128)(2,1)}), bf16[32,8,2048]{2,1,0:T(8,128)(2,1)S(1)}, u32[]{:S(2)}, u32[]{:S(2)}) async-start(bf16[32,8,2048]{2,1,0:T(8,128)(2,1)} %bitcast.2), calls=%async_computation.1 | async-start | bytes 2097152 | tf_op jit(solution)/shard_map/all_to_all | solution.py:126
  170.1 22.4 %all-to-all-start.5 = ((bf16[128,16,1,128]{0,3,2,1:T(8,128)(2,1)}), bf16[128,16,1,128]{0,3,2,1:T(8,128)(2,1)S(1)}, u32[]{:S(2)}, u32[]{:S(2)}) async-start(bf16[128,16,1,128]{0,3,2,1:T(8,128)(2,1)} %bitcast.18), calls=%async_computation.5 | async-start | bytes 1048576 | tf_op jit(solution)/shard_map/all_to_all | solution.py:155
  192.5 0.8 copy-start.3
  193.3 56.1 %all-to-all-start.9 = ((bf16[32,8,4096]{2,1,0:T(8,128)(2,1)}), bf16[32,8,4096]{2,1,0:T(8,128)(2,1)S(1)}, u32[]{:S(2)}, u32[]{:S(2)}) async-start(bf16[32,8,4096]{2,1,0:T(8,128)(2,1)} %bitcast.148), calls=%async_computation.9 | async-start | bytes 4194304 | tf_op jit(solution)/shard_map/all_to_all | solution.py:122
  249.3 20.4 %all-to-all-start.2 = ((bf16[128,16,1,128]{0,3,2,1:T(8,128)(2,1)}), bf16[128,16,1,128]{0,3,2,1:T(8,128)(2,1)}, u32[]{:S(2)}, u32[]{:S(2)}) async-start(bf16[128,16,1,128]{0,3,2,1:T(8,128)(2,1)} %bitcast.5), calls=%async_computation.2 | async-start | bytes 1048576 | tf_op jit(solution)/shard_map/all_to_all | solution.py:158
  255.6 4.0 copy-start.6
  255.6 4.0 copy-start.7
  259.2 16.9 %copy-start.1 = (bf16[128,4096]{1,0:T(8,128)(2,1)}, bf16[128,4096]{1,0:T(8,128)(2,1)S(1)}, u32[]{:S(2)}) copy-start(bf16[128,4096]{1,0:T(8,128)(2,1)S(1)} %scatter_custom_fusion.10) | copy-start | bytes 3145732
  259.2 15.8 %copy-start.4 = (bf16[128,16,1,128]{0,3,2,1:T(8,128)(2,1)S(1)}, bf16[128,16,1,128]{0,3,2,1:T(8,128)(2,1)}, u32[]{:S(2)}) copy-start(bf16[128,16,1,128]{0,3,2,1:T(8,128)(2,1)} %copy-done.3) | copy-start | bytes 1572868
  270.6 19.1 %all-to-all-start.10 = ((bf16[128,16,1,128]{3,0,2,1:T(8,128)(2,1)}), bf16[128,16,1,128]{3,0,2,1:T(8,128)(2,1)}, u32[]{:S(2)}, u32[]{:S(2)}) async-start(bf16[128,16,1,128]{3,0,2,1:T(8,128)(2,1)} %bitcast.32), calls=%async_computation.10 | async-start | bytes 1048576 | tf_op jit(solution)/shard_map/all_to_all | solution.py:157
  328.6 21.5 %all-to-all-start.12 = ((bf16[16,2,8192]{2,1,0:T(2,128)(2,1)}), bf16[16,2,8192]{2,1,0:T(2,128)(2,1)S(1)}, u32[]{:S(2)}, u32[]{:S(2)}) async-start(bf16[16,2,8192]{2,1,0:T(2,128)(2,1)} %reshape.266), calls=%async_computation.12 | async-start | bytes 1048576 | tf_op jit(solution)/shard_map/all_to_all | solution.py:164
  350.0 20.2 %all-to-all-start.11 = ((bf16[16,2,8192]{2,1,0:T(2,128)(2,1)}), bf16[16,2,8192]{2,1,0:T(2,128)(2,1)S(1)}, u32[]{:S(2)}, u32[]{:S(2)}) async-start(bf16[16,2,8192]{2,1,0:T(2,128)(2,1)} %reshape.264), calls=%async_computation.11 | async-start | bytes 1048576 | tf_op jit(solution)/shard_map/all_to_all | solution.py:163
  353.5 1.2 copy-start.2
  353.5 271.3 %all-reduce.2.cloned.1.call-start = ((), (), s32[]{:S(2)}) async-start(), calls=%async_computation.13 | async-start | bytes 524288 | tf_op jit(solution)/shard_map/psum | solution.py:186
Sparse Core Ops, SparseCore 0:
  359.9 264.8 all-reduce.1
where the time goes:
time: 635 us; the launch traced here: 633 us
  waiting for transfers between devices  349 us (55%)
  blocking collectives  119 us (19%)
  starting transfers between devices  60.9 us (10%)
  local copies, waits for them, and re-layouts  48.8 us (8%)
  matrix products  26.3 us (4%)
  between operations  14.3 us (2%)
  other arithmetic  12.2 us (2%)
    psum x1, waiting for transfers between devices, shards(): totals = lax.psum((grad_down_part, up_gradient_part), ('dp', 'seq'))  156 us
    psum x1, blocking collectives, shards(): totals = lax.psum((grad_down_part, up_gradient_part), ('dp', 'seq'))  96.7 us
    all_to_all x1, waiting for transfers between devices, shards(): lax.all_to_all(pack(hidden), 'dp', split_axis=0, concat_axis=0, tiled=True)  45.8 us
    all_to_all x1, waiting for transfers between devices, shards(): lax.all_to_all(pack(frozen_query), 'dp', split_axis=0, concat_axis=0, til...  24.2 us
    all_to_all x1, waiting for transfers between devices, shards(): lax.all_to_all(pack(upstream), 'dp', split_axis=0, concat_axis=0, tiled=T...  24.1 us
    all_to_all x1, blocking collectives, shards(): lax.all_to_all(send_label, 'dp', split_axis=0, concat_axis=0, tiled=True)  22.1 us
    scatter x7, local copies, waits for them, and re-layouts, settle(): return jnp.zeros((row_count,) + row_entries.shape[1:], row_entries.dtype)...  15.2 us
    scatter x5, local copies, waits for them, and re-layouts, pack(): return jnp.zeros((slot_total,) + row_entries.shape[1:], row_entries.dtype...  14.5 us
  transfers between devices with their start and end apart: 13, of which 13 were waited for; matrix products, arithmetic and copies ran while one was open for 7% of the time, Pallas kernels for 0%

commit v1 on v0

v1 whole, which is shorter than its diff:
```python
import functools
import math

import jax
import jax.numpy as jnp
from jax import lax
from jax.experimental import pallas as pl
from jax.experimental.pallas import tpu as pltpu
from jax.sharding import PartitionSpec as P

MESH = pl.DeviceIdType.MESH
BF = jnp.bfloat16
F32 = jnp.float32
HEAD = 128
RANK = 16
KV = 4
RATIO = 4
ONE_LANE = 16
SLOT_LANE = 17
DOC_LANE = 18


def mm(a, b):
    return jnp.dot(a, b, preferred_element_type=F32)


def mm_t(a, b):
    return lax.dot_general(a, b, (((1,), (1,)), ((), ())), preferred_element_type=F32)


def t_mm(a, b):
    return lax.dot_general(a, b, (((0,), (0,)), ((), ())), preferred_element_type=F32)


def iota(shape, dim):
    return lax.broadcasted_iota(jnp.int32, shape, dim)


def kernel(
    ndp,
    nx,
    nseq,
    hops,
    hidden_ref,
    q_ref,
    k_ref,
    v_ref,
    up_ref,
    group_ref,
    slot_ref,
    label_ref,
    down_ref,
    upw_ref,
    att_ref,
    gdown_ref,
    upg_ref,
    sa0,
    sb0,
    sa1,
    sb1,
    ra0,
    rb0,
    ra1,
    rb1,
    wa,
    wb,
    pbuf,
    bias,
    aret,
    sret,
    rret,
    srg,
    rrg,
    rgs,
    rgr,
    ar_s,
    ar_r,
    z_r,
    x_r,
    ag_r,
    dp_send,
    dp_recv,
    ring_send,
    ring_recv,
    sib_send,
    sib_recv,
    rg_send,
    rg_recv,
    ar_send,
    ar_recv,
    pack,
    unpack,
    unpack_t,
    value_ref,
):
    tok = hidden_ref.shape[0]
    nz = ndp // nx
    ny = nseq // 2
    cap = 2 * tok // ndp
    blk = 2 * cap
    slots = ndp * blk
    back = 2 * hops
    win = (back + 1) * tok
    d = lax.axis_index("dp")
    s = lax.axis_index("seq")
    z, x = d // nx, d % nx
    y, c = s // 2, s % 2
    stride = 13 if ndp == 32 else 1

    def dp_peer(step):
        off = (step * stride) % ndp
        return ((z + off // nx) % nz) * nx + (x + off % nx) % nx

    def seq_peer(step):
        return (s + step) % nseq

    barrier = pltpu.get_barrier_semaphore()

    def greet_dp(step, carry):
        pl.semaphore_signal(barrier, inc=1, device_id=(dp_peer(step), s), device_id_type=MESH)
        return carry

    def greet_seq(step, carry):
        pl.semaphore_signal(barrier, inc=1, device_id=(d, seq_peer(step)), device_id_type=MESH)
        return carry

    lax.fori_loop(1, ndp, greet_dp, 0)
    lax.fori_loop(1, nseq, greet_seq, 0)

    def rows_of(index, size):
        return pl.ds(pl.multiple_of(index * size, size), size)

    def send_dp(src, dst, kind):
        def step(i, carry):
            p = dp_peer(i)
            pltpu.make_async_remote_copy(
                src_ref=src.at[rows_of(p, blk)],
                dst_ref=dst.at[rows_of(d, blk)],
                send_sem=dp_send.at[kind],
                recv_sem=dp_recv.at[kind],
                device_id=(p, s),
                device_id_type=MESH,
            ).start()
            return carry

        lax.fori_loop(1, ndp, step, 0)
        here = rows_of(d, blk)
        pltpu.make_async_copy(src.at[here], dst.at[here], dp_recv.at[kind]).start()

    def wait_bytes(ref, sem):
        pltpu.make_async_copy(ref, ref, sem).wait()

    def wait_sent(ref, sem):
        wait_bytes(ref.at[pl.ds(0, slots - blk)], sem)

    lane = iota((tok, tok), 1)
    sub = iota((tok, tok), 0)
    grow = jnp.broadcast_to(group_ref[...].astype(F32), (tok, tok))
    same = (grow == grow.T) & (sub < lane)
    rank = jnp.sum(jnp.where(same, 1.0, 0.0), axis=0, keepdims=True)
    place = group_ref[...].astype(F32) * cap + rank
    srow = iota((slots, tok), 0)
    half_row = (srow % blk) // cap
    slot_id = ((srow // blk) * cap + srow % cap).astype(F32)
    hit = slot_id == place
    for f in range(2):
        pack[:, f * tok : (f + 1) * tok] = jnp.where(hit & (half_row == f), 1.0, 0.0).astype(BF)

    down = jnp.concatenate(
        [down_ref[...], jnp.zeros((HEAD - RANK, down_ref.shape[1]), BF)], axis=0
    )
    reduced = mm_t(hidden_ref[...], down).astype(BF)
    upw = upw_ref[...]
    upw_full = jnp.concatenate([upw, jnp.zeros((HEAD - RANK, upw.shape[1]), BF)], axis=0)
    value = (v_ref[...].astype(F32) + 2.0 * mm(reduced, upw_full)).astype(BF)
    value_ref[...] = value
    slot_col = jnp.broadcast_to(slot_ref[...].astype(F32), (tok, tok)).T
    tile = (reduced.astype(F32) + jnp.where(lane == SLOT_LANE, slot_col + 1.0, 0.0)).astype(BF)

    def kv_cols(rows, cc):
        return rows[:, cc * HEAD : (cc + 1) * HEAD]

    keys = k_ref[...]
    xa0 = jnp.concatenate(
        [
            jnp.concatenate([kv_cols(keys, 2 * f), kv_cols(value, 2 * f), tile], axis=1)
            for f in range(2)
        ],
        axis=0,
    )
    sa0[...] = mm(pack[...], xa0).astype(BF)

    pl.semaphore_wait(barrier, ndp + nseq - 2)
    send_dp(sa0, ra0, 0)

    keys = k_ref[...]
    value = value_ref[...]
    xb0 = jnp.concatenate(
        [
            jnp.concatenate([kv_cols(keys, 2 * f + 1), kv_cols(value, 2 * f + 1)], axis=1)
            for f in range(2)
        ],
        axis=0,
    )
    sb0[...] = mm(pack[...], xb0).astype(BF)
    send_dp(sb0, rb0, 1)

    half_heads = KV * RATIO // 2
    half_width = half_heads * HEAD
    diag = iota((HEAD, half_width), 0) // RANK == iota((HEAD, half_width), 1) // HEAD
    narrow = []
    for f in range(2):
        wide = jnp.concatenate(
            [kv_cols(upw, 2 * f + h // RATIO) for h in range(half_heads)], axis=1
        ).astype(F32)
        wide = jnp.concatenate([wide] * half_heads, axis=0)
        wide = jnp.where(diag, wide, 0.0).astype(BF)
        narrow.append(mm_t(up_ref[:, f * half_width : (f + 1) * half_width], wide).astype(BF))
    quad = RATIO * HEAD

    def q_cols(cc):
        return q_ref[:, cc * quad : (cc + 1) * quad]

    xa1 = jnp.concatenate(
        [jnp.concatenate([q_cols(2 * f), narrow[f]], axis=1) for f in range(2)], axis=0
    )
    sa1[...] = mm(pack[...], xa1).astype(BF)
    send_dp(sa1, ra1, 2)
    xb1 = jnp.concatenate([q_cols(2 * f + 1) for f in range(2)], axis=0)
    sb1[...] = mm(pack[...], xb1).astype(BF)
    send_dp(sb1, rb1, 3)

    def place_of(hop, core):
        return rows_of((hops - hop) * 2 + core, tok)

    def ring(piece, buf, hop):
        return pltpu.make_async_remote_copy(
            src_ref=buf.at[place_of(hop - 1, c)],
            dst_ref=buf.at[place_of(hop, c)],
            send_sem=ring_send.at[piece, hop],
            recv_sem=ring_recv.at[piece, hop],
            device_id=(d, ((y + 1) % ny) * 2 + c),
            device_id_type=MESH,
        )

    def sibling(piece, buf, hop):
        return pltpu.make_async_remote_copy(
            src_ref=buf.at[place_of(hop, c)],
            dst_ref=buf.at[place_of(hop, c)],
            send_sem=sib_send.at[piece, hop],
            recv_sem=sib_recv.at[piece, hop],
            device_id=(d, y * 2 + 1 - c),
            device_id_type=MESH,
        )

    def sibling_arrived(piece, buf, hop):
        wait_bytes(buf.at[place_of(hop, 1 - c)], sib_recv.at[piece, hop])

    wait_bytes(ra0, dp_recv.at[0])
    got = ra0[...]
    slot_in = jnp.broadcast_to(
        got[:, 2 * HEAD + SLOT_LANE : 2 * HEAD + SLOT_LANE + 1].astype(F32), (slots, tok)
    )
    at = slot_in == (iota((slots, tok), 1) + 1).astype(F32)
    for f in range(2):
        chosen = jnp.where(at & (half_row == f), 1.0, 0.0)
        unpack[:, f * tok : (f + 1) * tok] = chosen.astype(BF)
        unpack_t[f * tok : (f + 1) * tok, :] = chosen.T.astype(BF)
    arranged = mm(unpack_t[...], got).astype(BF)
    doc_col = jnp.broadcast_to(label_ref[...].astype(F32), (tok, tok)).T
    doc = lane.astype(F32) == doc_col + float(DOC_LANE)
    own_tile = arranged[:tok, 2 * HEAD :].astype(F32)
    own_tile = jnp.where((lane == ONE_LANE) | doc, 1.0, own_tile).astype(BF)
    own = place_of(0, c)
    wa[own, :] = jnp.concatenate(
        [arranged[:tok, : 2 * HEAD], arranged[tok:, : 2 * HEAD], own_tile], axis=1
    )
    ring(0, wa, 1).start()
    sibling(0, wa, 0).start()
    wait_bytes(rb0, dp_recv.at[1])
    arranged = mm(unpack_t[...], rb0[...]).astype(BF)
    wb[own, :] = jnp.concatenate([arranged[:tok, :], arranged[tok:, :]], axis=1)
    ring(1, wb, 1).start()
    sibling(1, wb, 0).start()
    for hop in range(1, hops + 1):
        for piece, buf in enumerate((wa, wb)):
            ring(piece, buf, hop).wait_recv()
            if hop < hops:
                ring(piece, buf, hop + 1).start()
            sibling(piece, buf, hop).start()
    for hop in range(hops + 1):
        for piece, buf in enumerate((wa, wb)):
            sibling_arrived(piece, buf, hop)

    window = rows_of(c, tok)
    window = pl.ds(window.start, win)
    tiles = wa[window, 4 * HEAD :]
    doc_q = jnp.where(doc, 1.0, 0.0).astype(BF)
    together = mm_t(doc_q, tiles) > 0.5
    col = iota((tok, win), 1)
    seen = together & (col - back * tok <= iota((tok, win), 0)) & (col >= (back - s) * tok)
    bias[...] = jnp.where(seen, 0.0, -1e30)
    scale = math.log2(math.e) / math.sqrt(HEAD)

    rg_total = jnp.zeros((RANK, win), F32)
    narrow_in = []
    returned = [jnp.zeros((tok, HEAD), F32) for _ in range(2)]
    for piece, (buf, arrived) in enumerate(((wa, ra1), (wb, rb1))):
        wait_bytes(arrived, dp_recv.at[2 + piece])
        arranged = mm(unpack_t[...], arrived[...]).astype(BF)
        if piece == 0:
            narrow_in = [arranged[f * tok : (f + 1) * tok, quad:].astype(F32) for f in range(2)]
        for f in range(2):
            cc = 2 * f + piece
            key = buf[window, 2 * f * HEAD : (2 * f + 1) * HEAD]
            val = jnp.concatenate(
                [buf[window, (2 * f + 1) * HEAD : (2 * f + 2) * HEAD], tiles], axis=1
            )
            lefts = []
            for h in range(RATIO):
                head = cc * RATIO + h
                lanes = (piece * RATIO + h) * RANK
                query = arranged[f * tok : (f + 1) * tok, h * HEAD : (h + 1) * HEAD]
                scores = mm_t(query, key) * scale + bias[...]
                top = jnp.max(scores, axis=1, keepdims=True)
                weights = jnp.exp2(scores - top).astype(BF)
                pbuf[h * tok : (h + 1) * tok, :] = weights
                out = mm(weights, val)
                inv = 1.0 / out[:, HEAD + ONE_LANE : HEAD + ONE_LANE + 1]
                att_ref[:, head * HEAD : (head + 1) * HEAD] = (out[:, :HEAD] * inv).astype(BF)
                mixed = jnp.where(lane < RANK, out[:, HEAD:] * inv, 0.0)
                returned[f] = returned[f] + (pltpu.roll(mixed, lanes, 1) if lanes else mixed)
                left = narrow_in[f]
                left = pltpu.roll(left, HEAD - lanes, 1) if lanes else left
                lefts.append((left[:, :RANK] * inv).astype(BF))
            rg_total = rg_total + t_mm(jnp.concatenate(lefts, axis=0), pbuf[...])

    aret[:tok, :] = returned[0].astype(BF)
    aret[tok:, :] = returned[1].astype(BF)
    sret[...] = mm(unpack[...], aret[...]).astype(BF)
    send_dp(sret, rret, 4)

    def rg_copy(w):
        return pltpu.make_async_remote_copy(
            src_ref=rgs.at[w * RANK : (w + 1) * RANK],
            dst_ref=rgr.at[w * RANK : (w + 1) * RANK],
            send_sem=rg_send.at[w],
            recv_sem=rg_recv.at[w],
            device_id=(d, (s + nseq - back + w) % nseq),
            device_id_type=MESH,
        )

    for w in range(back):
        rgs[w * RANK : (w + 1) * RANK, :] = rg_total[:, w * tok : (w + 1) * tok].astype(BF)
    for w in range(back):
        rg_copy(w).start()
    rg_own = rg_total[:, back * tok :]
    for w in range(back):
        rg_copy(w).wait_recv()
        rg_own = rg_own + rgr[w * RANK : (w + 1) * RANK, :].astype(F32)
    rg_pad = jnp.concatenate(
        [(2.0 * rg_own).astype(BF), jnp.zeros((HEAD - RANK, tok), BF)], axis=0
    )
    srg[...] = mm_t(unpack[:, :tok], rg_pad).astype(BF)
    send_dp(srg, rrg, 5)

    share = ar_s.shape[2] // HEAD

    def put(col, rows):
        lanes = (col % share) * HEAD
        ar_s[col // share, :, lanes : lanes + HEAD] = rows

    n_down = hidden_ref.shape[1] // HEAD
    wait_bytes(rret, dp_recv.at[4])
    mixed = t_mm(pack[...], rret[...]).astype(BF)
    for f in range(2):
        full = t_mm(
            mixed[f * tok : (f + 1) * tok, :], up_ref[:, f * half_width : (f + 1) * half_width]
        )
        for g in range(2):
            total = jnp.zeros((RANK, HEAD), F32)
            for h in range(g * RATIO, (g + 1) * RATIO):
                total = total + full[h * RANK : (h + 1) * RANK, h * HEAD : (h + 1) * HEAD]
            put(n_down + 2 * f + g, 2.0 * total)
    wait_bytes(rrg, dp_recv.at[5])
    rg_rows = t_mm(pack[:, :tok], rrg[...]).astype(BF)
    grad = t_mm(rg_rows[:, :RANK], hidden_ref[...])
    for t in range(n_down):
        put(t, grad[:, t * HEAD : (t + 1) * HEAD])

    def ar_start(phase, src, dst, target):
        pltpu.make_async_remote_copy(
            src_ref=src,
            dst_ref=dst,
            send_sem=ar_send.at[phase],
            recv_sem=ar_recv.at[phase],
            device_id=target,
            device_id_type=MESH,
        ).start()

    def total_of(buf, n):
        total = buf[0]
        for i in range(1, n):
            total = total + buf[i]
        return total

    def scatter(i, carry):
        p = seq_peer(i)
        ar_start(0, ar_s.at[p], ar_r.at[s], (d, p))
        return carry

    lax.fori_loop(1, nseq, scatter, 0)
    ar_r[s] = ar_s[s]
    wait_bytes(ar_r.at[pl.ds(0, nseq - 1)], ar_recv.at[0])
    z_r[z] = total_of(ar_r, nseq)

    def over_z(i, carry):
        ar_start(1, z_r.at[z], z_r.at[z], (((z + i) % nz) * nx + x, s))
        return carry

    lax.fori_loop(1, nz, over_z, 0)
    wait_bytes(z_r.at[pl.ds(0, nz - 1)], ar_recv.at[1])
    x_r[x] = total_of(z_r, nz)

    def over_x(i, carry):
        ar_start(2, x_r.at[x], x_r.at[x], (z * nx + (x + i) % nx, s))
        return carry

    lax.fori_loop(1, nx, over_x, 0)
    wait_bytes(x_r.at[pl.ds(0, nx - 1)], ar_recv.at[2])
    ag_r[s] = total_of(x_r, nx)

    def gather(i, carry):
        ar_start(3, ag_r.at[s], ag_r.at[s], (d, seq_peer(i)))
        return carry

    lax.fori_loop(1, nseq, gather, 0)
    wait_bytes(ag_r.at[pl.ds(0, nseq - 1)], ar_recv.at[3])
    for t in range(n_down + KV):
        lanes = (t % share) * HEAD
        out, col = (gdown_ref, t) if t < n_down else (upg_ref, t - n_down)
        out[:, col * HEAD : (col + 1) * HEAD] = ag_r[t // share, :, lanes : lanes + HEAD]

    for kind, buf in enumerate((sa0, sb0, sa1, sb1, sret, srg)):
        wait_sent(buf, dp_send.at[kind])
    for piece, buf in enumerate((wa, wb)):
        for hop in range(1, hops + 1):
            ring(piece, buf, hop).wait_send()
        for hop in range(hops + 1):
            sibling(piece, buf, hop).wait_send()
    for w in range(back):
        rg_copy(w).wait_send()
    wait_bytes(ar_s.at[pl.ds(0, nseq - 1)], ar_send.at[0])
    wait_bytes(z_r.at[pl.ds(0, nz - 1)], ar_send.at[1])
    wait_bytes(x_r.at[pl.ds(0, nx - 1)], ar_send.at[2])
    wait_bytes(ag_r.at[pl.ds(0, nseq - 1)], ar_send.at[3])


def shards(nx, hops, hidden, q, k, v, up, group, slot, labels, down, upw):
    ndp = lax.axis_size("dp")
    nseq = lax.axis_size("seq")
    tok = hidden.shape[0]
    slots = 4 * tok
    back = 2 * hops
    n_tiles = (hidden.shape[1] + upw.shape[1]) // HEAD
    share = -(-n_tiles // nseq) * HEAD
    dma = pltpu.SemaphoreType.DMA
    la0, lb0, la1, lb1 = 3 * HEAD, 2 * HEAD, 5 * HEAD, 4 * HEAD
    scratch = (
        [pltpu.VMEM((slots, n), BF) for n in (la0, lb0, la1, lb1)]
        + [pltpu.VMEM((slots, n), BF) for n in (la0, lb0, la1, lb1)]
        + [
            pltpu.VMEM(((back + 2) * tok, 5 * HEAD), BF),
            pltpu.VMEM(((back + 2) * tok, 4 * HEAD), BF),
            pltpu.VMEM((RATIO * tok, (back + 1) * tok), BF),
            pltpu.VMEM((tok, (back + 1) * tok), F32),
            pltpu.VMEM((2 * tok, HEAD), BF),
        ]
        + [pltpu.VMEM((slots, HEAD), BF)] * 4
        + [pltpu.VMEM((back * RANK, tok), BF)] * 2
        + [
            pltpu.VMEM((nseq, RANK, share), F32),
            pltpu.VMEM((nseq, RANK, share), F32),
            pltpu.VMEM((ndp // nx, RANK, share), F32),
            pltpu.VMEM((nx, RANK, share), F32),
            pltpu.VMEM((nseq, RANK, share), F32),
            dma((6,)),
            dma((6,)),
            dma((2, hops + 1)),
            dma((2, hops + 1)),
            dma((2, hops + 1)),
            dma((2, hops + 1)),
            dma((back,)),
            dma((back,)),
            dma((4,)),
            dma((4,)),
            pltpu.VMEM((slots, 2 * tok), BF),
            pltpu.VMEM((slots, 2 * tok), BF),
            pltpu.VMEM((2 * tok, slots), BF),
            pltpu.VMEM((tok, KV * HEAD), BF),
        ]
    )
    vmem = pl.BlockSpec(memory_space=pltpu.VMEM)
    return pl.pallas_call(
        functools.partial(kernel, ndp, nx, nseq, hops),
        out_shape=(
            jax.ShapeDtypeStruct(q.shape, BF),
            jax.ShapeDtypeStruct(down.shape, F32),
            jax.ShapeDtypeStruct(upw.shape, F32),
        ),
        in_specs=[vmem] * 10,
        out_specs=(vmem, vmem, vmem),
        scratch_shapes=scratch,
        compiler_params=pltpu.CompilerParams(
            collective_id=0, has_side_effects=True, vmem_limit_bytes=56 * 1024 * 1024
        ),
        cost_estimate=pl.CostEstimate(
            flops=4 * 10**9, bytes_accessed=4 * 10**6, transcendentals=2400000
        ),
    )(
        hidden,
        q,
        k,
        v,
        up,
        group.reshape(1, tok),
        slot.reshape(1, tok),
        labels,
        down,
        upw,
    )


def build(mesh, nx, hops):
    rows = P(("dp", "seq"), None)
    return jax.shard_map(
        functools.partial(shards, nx, hops),
        mesh=mesh,
        in_specs=(
            rows,
            rows,
            rows,
            rows,
            rows,
            P(("dp", "seq")),
            P(("dp", "seq")),
            P("dp", "seq"),
            P(),
            P(),
        ),
        out_specs=(rows, P(), P()),
        check_vma=False,
    )


def solution(mesh):
    return build(mesh, 4, 4)
```

time: 635 us -> 120 us (0.19)
  waiting for transfers between devices: 349 us -> 0 us
  blocking collectives: 119 us -> 0 us
  Pallas kernels: 0 us -> 116 us
  starting transfers between devices: 60.9 us -> 0 us
  local copies, waits for them, and re-layouts: 48.8 us -> 3.3 us
  matrix products: 26.3 us -> 0 us
  between operations: 14.3 us -> 0.65 us
  other arithmetic: 12.2 us -> 0 us
    all_to_all x12 -> x0, waiting for transfers between devices: 193 us -> none  [the longest x1 45.8 us: shards(): lax.all_to_all(pack(hidden), 'dp', split_axis=0, concat_axis=0, tiled=True)]
    psum x1 -> x0, waiting for transfers between devices: 156 us -> none  [shards(): totals = lax.psum((grad_down_part, up_gradient_part), ('dp', 'seq'))]
    pallas_call x0 -> x1, Pallas kernels: none -> 116 us  [shards(): pl.pallas_call(functools.partial(kernel, ndp, nx, nseq, hops), out_shape=...]
    psum x1 -> x0, blocking collectives: 96.7 us -> none  [shards(): totals = lax.psum((grad_down_part, up_gradient_part), ('dp', 'seq'))]
    all_to_all x12 -> x0, starting transfers between devices: 60.8 us -> none  [the longest x1 9.22 us: shards(): lax.all_to_all(labels, 'seq', split_axis=1, concat_axis=0, tiled=True)]
    scatter x13 -> x0, local copies, waits for them, and re-layouts: 30.9 us -> none  [the longest x7 15.2 us: settle(): return jnp.zeros((row_count,) + row_entries.shape[1:], row_entries.dtype)...]
    dot_general x16 -> x0, matrix products: 26.3 us -> none  [the longest x4 9.65 us: block_step(): jnp.einsum('hqk,khd->qhd', attn_weights, value_heads, preferred_element_t...]
    all_to_all x1 -> x0, blocking collectives: 22.1 us -> none  [shards(): lax.all_to_all(send_label, 'dp', split_axis=0, concat_axis=0, tiled=True)]
  transfers between devices with their start and end apart: 13 -> 0, of which waited for: 13 -> 0; matrix products, arithmetic and copies ran while one was open for 7% -> 0% of each run, Pallas kernels for 0% -> 0%
where the time goes in v1:
time: 120 us
  Pallas kernels  116 us (97%)
  local copies, waits for them, and re-layouts  3.3 us (3%)
    pallas_call x1, Pallas kernels, shards(): pl.pallas_call(functools.partial(kernel, ndp, nx, nseq, hops), out_shape=...  116 us
    unnamed x7, local copies, waits for them, and re-layouts  3.3 us

profile of v1, /device:TPU:1, one launch (start us, length us, event | category | flops | bytes accessed | tf_op | source)
XLA Modules:
  0.0 119.8 jit_solution(17533398699473882679)
XLA Ops:
  0.6 115.8 %shard_map.121 = (bf16[128,2048]{1,0:T(8,128)(2,1)}, f32[16,4096]{1,0:T(8,128)}, f32[16,512]{1,0:T(8,128)}) custom-call(bf16[128,4096]{1,0:T(8,128)(2,1)} %hidden_ref.1, bf16[128,2048]{1,0:T(8,128)(2,1)} %q_ref.1, bf16[128,512]{1,0:T(8,128)(2,1)} %k_ref.1, bf16[128,512]{1,0:T(8,128)(2,1)} %v_ref.1, bf16[128,2048]{1,0:T(8,128)(2,1)} %up_ref.1, ...), custom_call_target="tpu_custom_call" | custom-call | flops 4000000000 | bytes 4000000 | tf_op jit(solution)/shard_map/pallas_call | solution.py:504
  116.5 0.0 copy-start
  116.5 1.9 %copy.16 = bf16[128,2048]{1,0:T(8,128)(2,1)} copy(bf16[128,2048]{1,0:T(8,128)(2,1)} %get-tuple-element.6) | data formatting | bytes 1048576
  118.4 0.0 copy-done
  118.4 0.0 copy-start.1
  118.4 0.7 copy.17
  119.1 0.1 copy-done.1
  119.2 0.6 copy.18
Async XLA Ops:
  116.5 1.9 %copy-start = (f32[16,4096]{1,0:T(8,128)S(1)}, f32[16,4096]{1,0:T(8,128)}, u32[]{:S(2)}) copy-start(f32[16,4096]{1,0:T(8,128)} %get-tuple-element.7) | copy-start | bytes 786436
  118.4 0.8 copy-start.1

commit v2 on v1

v2 whole, which is shorter than its diff:
```python
import functools
import math

import jax
import jax.numpy as jnp
from jax import lax
from jax.experimental import pallas as pl
from jax.experimental.pallas import tpu as pltpu
from jax.sharding import PartitionSpec as P

MESH = pl.DeviceIdType.MESH
BF = jnp.bfloat16
F32 = jnp.float32
HEAD = 128
RANK = 16
KV = 4
RATIO = 4
ONE_LANE = 16
DOC_LANE = 17
SPAN = HEAD // RANK


def mm(a, b):
    return jnp.dot(a, b, preferred_element_type=F32)


def mm_t(a, b):
    return lax.dot_general(a, b, (((1,), (1,)), ((), ())), preferred_element_type=F32)


def t_mm(a, b):
    return lax.dot_general(a, b, (((0,), (0,)), ((), ())), preferred_element_type=F32)


def iota(shape, dim):
    return lax.broadcasted_iota(jnp.int32, shape, dim)


def kernel(
    ndp,
    nx,
    nseq,
    hops,
    hidden_in,
    q_in,
    k_in,
    v_in,
    up_in,
    group_ref,
    slot_ref,
    label_ref,
    down_ref,
    upw_ref,
    att_out,
    gdown_ref,
    upg_ref,
    sa0,
    sb0,
    sa1,
    sb1,
    sb2,
    ra0,
    rb0,
    ra1,
    rb1,
    rb2,
    wa,
    wb,
    pbuf,
    bias,
    aret,
    sret,
    rret,
    sx,
    rx,
    srg,
    rrg,
    rgs,
    rgr,
    g_s,
    g_r,
    g_t,
    g_a,
    u_s,
    u_r,
    u_t,
    u_a,
    dp_send,
    dp_recv,
    ring_send,
    ring_recv,
    sib_send,
    sib_recv,
    rg_send,
    rg_recv,
    ar_send,
    ar_recv,
    u_send,
    u_recv,
    small,
    unsmall,
    pack,
    unpack,
    unpack_t,
    value_ref,
    hidden_ref,
    q_ref,
    k_ref,
    v_ref,
    up_ref,
    att_ref,
    load,
):
    tok = hidden_ref.shape[0]
    loads = [
        pltpu.make_async_copy(src, dst, load.at[i])
        for i, (src, dst) in enumerate(
            (
                (hidden_in, hidden_ref),
                (k_in, k_ref),
                (v_in, v_ref),
                (q_in, q_ref),
                (up_in, up_ref),
            )
        )
    ]
    att_copy = pltpu.make_async_copy(att_ref, att_out, load.at[5])
    for copy in loads:
        copy.start()
    nz = ndp // nx
    ny = nseq // 2
    cap = 2 * tok // ndp
    blk = 2 * cap
    slots = ndp * blk
    back = 2 * hops
    win = (back + 1) * tok
    d = lax.axis_index("dp")
    s = lax.axis_index("seq")
    z, x = d // nx, d % nx
    y, c = s // 2, s % 2
    stride = 13 if ndp == 32 else 1

    def dp_peer(step):
        off = (step * stride) % ndp
        return ((z + off // nx) % nz) * nx + (x + off % nx) % nx

    def seq_peer(step):
        return (s + step) % nseq

    barrier = pltpu.get_barrier_semaphore()

    def greet_dp(step, carry):
        pl.semaphore_signal(barrier, inc=1, device_id=(dp_peer(step), s), device_id_type=MESH)
        return carry

    def greet_seq(step, carry):
        pl.semaphore_signal(barrier, inc=1, device_id=(d, seq_peer(step)), device_id_type=MESH)
        return carry

    lax.fori_loop(1, ndp, greet_dp, 0)
    lax.fori_loop(1, nseq, greet_seq, 0)

    def rows_of(index, size):
        return pl.ds(pl.multiple_of(index * size, size), size)

    def send_dp(src, dst, kind, size=blk):
        def step(i, carry):
            p = dp_peer(i)
            pltpu.make_async_remote_copy(
                src_ref=src.at[rows_of(p, size)],
                dst_ref=dst.at[rows_of(d, size)],
                send_sem=dp_send.at[kind],
                recv_sem=dp_recv.at[kind],
                device_id=(p, s),
                device_id_type=MESH,
            ).start()
            return carry

        lax.fori_loop(1, ndp, step, 0)
        here = rows_of(d, size)
        pltpu.make_async_copy(src.at[here], dst.at[here], dp_recv.at[kind]).start()

    def wait_bytes(ref, sem):
        pltpu.make_async_copy(ref, ref, sem).wait()

    def wait_sent(ref, sem, size=blk):
        wait_bytes(ref.at[pl.ds(0, (ndp - 1) * size)], sem)

    lane = iota((tok, tok), 1)
    sub = iota((tok, tok), 0)
    grow = jnp.broadcast_to(group_ref[...].astype(F32), (tok, tok))
    same = (grow == grow.T) & (sub < lane)
    rank = jnp.sum(jnp.where(same, 1.0, 0.0), axis=0, keepdims=True)
    place = group_ref[...].astype(F32) * cap + rank
    srow = iota((slots, tok), 0)
    half_row = (srow % blk) // cap
    slot_id = ((srow // blk) * cap + srow % cap).astype(F32)
    hit = slot_id == place
    for f in range(2):
        pack[:, f * tok : (f + 1) * tok] = jnp.where(hit & (half_row == f), 1.0, 0.0).astype(BF)

    n_small = slots // 2
    lines = n_small // SPAN
    per_peer = lines // ndp
    mine = iota((n_small, HEAD), 1) // RANK == iota((n_small, HEAD), 0) % SPAN

    def to_lines(rows):
        kept = jnp.where(mine, rows, 0.0).reshape(lines, SPAN, HEAD)
        return jnp.sum(kept, axis=1, keepdims=True)

    def from_lines(line):
        spread = jnp.broadcast_to(line, (lines, SPAN, HEAD)).reshape(n_small, HEAD)
        return jnp.where(mine, spread, 0.0)

    fold = (sub % RANK == lane) & (lane < RANK)
    fold = jnp.where(fold, 1.0, 0.0).astype(BF)
    small_id = iota((n_small, tok), 0).astype(F32)
    small[...] = jnp.where(small_id == place, 1.0, 0.0).astype(BF)

    down = jnp.concatenate([down_ref[...]] * SPAN, axis=0)
    loads[0].wait()
    reduced = mm_t(hidden_ref[...], down).astype(BF)
    upw = upw_ref[...]
    upw_full = jnp.concatenate([upw, jnp.zeros((HEAD - RANK, upw.shape[1]), BF)], axis=0)
    loads[2].wait()
    value = (v_ref[...].astype(F32) + 2.0 * mm(reduced, upw_full)).astype(BF)
    value_ref[...] = value
    slot_col = jnp.broadcast_to(slot_ref[...].astype(F32), (tok, tok)).T
    sx[:, 0:1, :] = to_lines(mm(small[...], reduced))
    sx[:, 1:2, :] = to_lines(mm(small[...], (slot_col + 1.0).astype(BF)))

    def kv_cols(rows, cc):
        return rows[:, cc * HEAD : (cc + 1) * HEAD]

    loads[1].wait()
    keys = k_ref[...]
    xa0 = jnp.concatenate(
        [
            jnp.concatenate([kv_cols(keys, 2 * f), kv_cols(value, 2 * f)], axis=1)
            for f in range(2)
        ],
        axis=0,
    )
    sa0[...] = mm(pack[...], xa0).astype(BF)

    pl.semaphore_wait(barrier, ndp + nseq - 2)
    send_dp(sx, rx, 6, per_peer)
    send_dp(sa0, ra0, 0)

    keys = k_ref[...]
    value = value_ref[...]
    xb0 = jnp.concatenate(
        [
            jnp.concatenate([kv_cols(keys, 2 * f + 1), kv_cols(value, 2 * f + 1)], axis=1)
            for f in range(2)
        ],
        axis=0,
    )
    sb0[...] = mm(pack[...], xb0).astype(BF)
    send_dp(sb0, rb0, 1)

    half_heads = KV * RATIO // 2
    half_width = half_heads * HEAD
    diag = iota((HEAD, half_width), 0) // RANK == iota((HEAD, half_width), 1) // HEAD
    narrow = []
    loads[4].wait()
    for f in range(2):
        wide = jnp.concatenate(
            [kv_cols(upw, 2 * f + h // RATIO) for h in range(half_heads)], axis=1
        ).astype(F32)
        wide = jnp.concatenate([wide] * half_heads, axis=0)
        wide = jnp.where(diag, wide, 0.0).astype(BF)
        narrow.append(mm_t(up_ref[:, f * half_width : (f + 1) * half_width], wide).astype(BF))
    quad = RATIO * HEAD

    def q_cols(cc):
        return q_ref[:, cc * quad : (cc + 1) * quad]

    loads[3].wait()
    xa1 = jnp.concatenate(
        [jnp.concatenate([q_cols(2 * f), narrow[f]], axis=1) for f in range(2)], axis=0
    )
    sa1[...] = mm(pack[...], xa1).astype(BF)
    send_dp(sa1, ra1, 2)
    xb1 = jnp.concatenate([q_cols(2 * f + 1) for f in range(2)], axis=0)
    sb1[...] = mm(pack[...], xb1[:, : quad // 2]).astype(BF)
    send_dp(sb1, rb1, 3)
    sb2[...] = mm(pack[...], xb1[:, quad // 2 :]).astype(BF)
    send_dp(sb2, rb2, 7)

    def place_of(hop, core):
        return rows_of((hops - hop) * 2 + core, tok)

    def ring(piece, buf, hop):
        return pltpu.make_async_remote_copy(
            src_ref=buf.at[place_of(hop - 1, c)],
            dst_ref=buf.at[place_of(hop, c)],
            send_sem=ring_send.at[piece, hop],
            recv_sem=ring_recv.at[piece, hop],
            device_id=(d, ((y + 1) % ny) * 2 + c),
            device_id_type=MESH,
        )

    def sibling(piece, buf, hop):
        return pltpu.make_async_remote_copy(
            src_ref=buf.at[place_of(hop, c)],
            dst_ref=buf.at[place_of(hop, c)],
            send_sem=sib_send.at[piece, hop],
            recv_sem=sib_recv.at[piece, hop],
            device_id=(d, y * 2 + 1 - c),
            device_id_type=MESH,
        )

    def sibling_arrived(piece, buf, hop):
        wait_bytes(buf.at[place_of(hop, 1 - c)], sib_recv.at[piece, hop])

    wait_bytes(rx, dp_recv.at[6])
    slot_in = jnp.max(from_lines(rx[:, 1:2, :]), axis=1, keepdims=True)
    slot_in = jnp.broadcast_to(slot_in, (n_small, tok))
    at_small = jnp.where(slot_in == (iota((n_small, tok), 1) + 1).astype(F32), 1.0, 0.0)
    unsmall[...] = at_small.astype(BF)
    at = jnp.broadcast_to(at_small.reshape(ndp, 1, cap, tok), (ndp, 2, cap, tok))
    at = at.reshape(slots, tok)
    for f in range(2):
        chosen = jnp.where(half_row == f, at, 0.0)
        unpack[:, f * tok : (f + 1) * tok] = chosen.astype(BF)
        unpack_t[f * tok : (f + 1) * tok, :] = chosen.T.astype(BF)
    reduced_in = t_mm(unsmall[...], from_lines(rx[:, 0:1, :]).astype(BF)).astype(BF)
    own_tile = mm(reduced_in, fold)
    wait_bytes(ra0, dp_recv.at[0])
    arranged = mm(unpack_t[...], ra0[...]).astype(BF)
    doc_col = jnp.broadcast_to(label_ref[...].astype(F32), (tok, tok)).T
    doc = lane.astype(F32) == doc_col + float(DOC_LANE)
    own_tile = jnp.where((lane == ONE_LANE) | doc, 1.0, own_tile).astype(BF)
    own = place_of(0, c)
    wa[own, :] = jnp.concatenate(
        [arranged[:tok, :], arranged[tok:, :], own_tile], axis=1
    )
    ring(0, wa, 1).start()
    sibling(0, wa, 0).start()
    wait_bytes(rb0, dp_recv.at[1])
    arranged = mm(unpack_t[...], rb0[...]).astype(BF)
    wb[own, :] = jnp.concatenate([arranged[:tok, :], arranged[tok:, :]], axis=1)
    ring(1, wb, 1).start()
    sibling(1, wb, 0).start()
    def pass_on(piece, buf, hop):
        ring(piece, buf, hop).wait_recv()
        if hop < hops:
            ring(piece, buf, hop + 1).start()
        sibling(piece, buf, hop).start()

    for hop in range(1, hops):
        pass_on(0, wa, hop)
        pass_on(1, wb, hop)
    wait_bytes(ra1, dp_recv.at[2])
    queries = mm(unpack_t[...], ra1[...]).astype(BF)
    pass_on(0, wa, hops)
    for hop in range(hops + 1):
        sibling_arrived(0, wa, hop)

    window = rows_of(c, tok)
    window = pl.ds(window.start, win)
    tiles = wa[window, 4 * HEAD :]
    doc_q = jnp.where(doc, 1.0, 0.0).astype(BF)
    together = mm_t(doc_q, tiles) > 0.5
    col = iota((tok, win), 1)
    seen = together & (col - back * tok <= iota((tok, win), 0)) & (col >= (back - s) * tok)
    bias[...] = jnp.where(seen, 0.0, -1e30)
    scale = math.log2(math.e) / math.sqrt(HEAD)

    narrow_in = [queries[f * tok : (f + 1) * tok, quad:].astype(F32) for f in range(2)]
    returned = [jnp.zeros((tok, HEAD), F32) for _ in range(2)]

    def attend(piece, buf, arranged, f, first, count):
        cc = 2 * f + piece
        key = buf[window, 2 * f * HEAD : (2 * f + 1) * HEAD]
        val = jnp.concatenate(
            [buf[window, (2 * f + 1) * HEAD : (2 * f + 2) * HEAD], tiles], axis=1
        )
        query = jnp.concatenate(
            [
                arranged[f * tok : (f + 1) * tok, h * HEAD : (h + 1) * HEAD]
                for h in range(count)
            ],
            axis=0,
        )
        scores = mm_t(query, key)
        for h in range(count):
            part = scores[h * tok : (h + 1) * tok, :] * scale + bias[...]
            top = jnp.max(part, axis=1, keepdims=True)
            pbuf[f, h * tok : (h + 1) * tok, :] = jnp.exp2(part - top).astype(BF)
        weights = pbuf[f, : count * tok, :]
        out = mm(weights, val)
        inv = 1.0 / out[:, HEAD + ONE_LANE : HEAD + ONE_LANE + 1]
        attended = (out[:, :HEAD] * inv).astype(BF)
        mixed = jnp.where(iota((count * tok, HEAD), 1) < RANK, out[:, HEAD:] * inv, 0.0)
        lefts = []
        for h in range(count):
            head = cc * RATIO + first + h
            lanes = (piece * RATIO + first + h) * RANK
            rows = slice(h * tok, (h + 1) * tok)
            att_ref[:, head * HEAD : (head + 1) * HEAD] = attended[rows]
            moved = pltpu.roll(mixed[rows], lanes, 1) if lanes else mixed[rows]
            returned[f] = returned[f] + moved
            left = narrow_in[f]
            left = pltpu.roll(left, HEAD - lanes, 1) if lanes else left
            lefts.append((left[:, :RANK] * inv[rows]).astype(BF))
        return t_mm(jnp.concatenate(lefts, axis=0), weights)

    half = RATIO // 2
    rg_total = attend(0, wa, queries, 0, 0, RATIO)
    pass_on(1, wb, hops)
    rg_total = rg_total + attend(0, wa, queries, 1, 0, RATIO)
    for hop in range(hops + 1):
        sibling_arrived(1, wb, hop)
    for arrived, kind, first in ((rb1, 3, 0), (rb2, 7, half)):
        wait_bytes(arrived, dp_recv.at[kind])
        queries = mm(unpack_t[...], arrived[...]).astype(BF)
        for f in range(2):
            rg_total = rg_total + attend(1, wb, queries, f, first, half)
    att_copy.start()

    def rg_copy(w):
        return pltpu.make_async_remote_copy(
            src_ref=rgs.at[w * RANK : (w + 1) * RANK],
            dst_ref=rgr.at[w * RANK : (w + 1) * RANK],
            send_sem=rg_send.at[w],
            recv_sem=rg_recv.at[w],
            device_id=(d, (s + nseq - back + w) % nseq),
            device_id_type=MESH,
        )

    for w in range(back):
        rgs[w * RANK : (w + 1) * RANK, :] = rg_total[:, w * tok : (w + 1) * tok].astype(BF)
    for w in range(back):
        rg_copy(w).start()
    rg_own = rg_total[:, back * tok :]

    aret[:tok, :] = returned[0].astype(BF)
    aret[tok:, :] = returned[1].astype(BF)
    sret[...] = mm(unpack[...], aret[...]).astype(BF)
    send_dp(sret, rret, 4)

    for w in range(back):
        rg_copy(w).wait_recv()
        rg_own = rg_own + rgr[w * RANK : (w + 1) * RANK, :].astype(F32)
    rg_own = jnp.concatenate([(2.0 * rg_own).astype(BF)] * SPAN, axis=0)
    srg[...] = to_lines(mm_t(unsmall[...], rg_own))
    send_dp(srg, rrg, 5, per_peer)

    def copy_start(src, dst, send, recv, target):
        pltpu.make_async_remote_copy(
            src_ref=src,
            dst_ref=dst,
            send_sem=send,
            recv_sem=recv,
            device_id=target,
            device_id_type=MESH,
        ).start()

    def to_seq(buf, send, recv):
        def step(i, carry):
            copy_start(buf.at[s], buf.at[s], send, recv, (d, seq_peer(i)))
            return carry

        lax.fori_loop(1, nseq, step, 0)

    def total_of(buf, n):
        parts = [buf[i].astype(F32) for i in range(n)]
        while len(parts) > 1:
            parts = [a + b for a, b in zip(parts[::2], parts[1::2])]
        return parts[0]

    wait_bytes(rret, dp_recv.at[4])
    mixed = t_mm(pack[...], rret[...]).astype(BF)
    for f in range(2):
        full = t_mm(
            mixed[f * tok : (f + 1) * tok, :], up_ref[:, f * half_width : (f + 1) * half_width]
        )
        for g in range(2):
            total = jnp.zeros((RANK, HEAD), F32)
            for h in range(g * RATIO, (g + 1) * RATIO):
                total = total + full[h * RANK : (h + 1) * RANK, h * HEAD : (h + 1) * HEAD]
            u_s[2 * f + g] = (2.0 * total).astype(BF)
    apart = ndp // KV
    owner = d % apart == 0
    for t in range(KV):

        @pl.when(d != t * apart)
        def _():
            copy_start(u_s.at[t], u_r.at[d], u_send.at[t], u_recv.at[0], (t * apart, s))

        @pl.when(d == t * apart)
        def _():
            pltpu.make_async_copy(u_s.at[t], u_r.at[d], u_recv.at[0]).start()

    n_share = g_s.shape[2]
    wait_bytes(rrg, dp_recv.at[5])
    rg_rows = t_mm(small[...], from_lines(rrg[...]).astype(BF)).astype(BF)
    rg_rows = mm(rg_rows, fold).astype(BF)
    grad = t_mm(rg_rows[:, :RANK], hidden_ref[...])
    for t in range(ndp):
        g_s[t] = grad[:, t * n_share : (t + 1) * n_share].astype(BF)

    def spread(src_of, dst, phase):
        def step(i, carry):
            p = dp_peer(i)
            copy_start(src_of(p), dst.at[d], ar_send.at[phase], ar_recv.at[phase], (p, s))
            return carry

        lax.fori_loop(1, ndp, step, 0)

    spread(lambda p: g_s.at[p], g_r, 0)
    pltpu.make_async_copy(g_s.at[d], g_r.at[d], ar_recv.at[0]).start()

    @pl.when(owner)
    def _():
        wait_bytes(u_r, u_recv.at[0])
        u_t[s] = total_of(u_r, ndp).astype(BF)
        to_seq(u_t, u_send.at[KV], u_recv.at[1])

    wait_bytes(g_r, ar_recv.at[0])
    g_t[s] = total_of(g_r, ndp).astype(BF)
    to_seq(g_t, ar_send.at[1], ar_recv.at[1])

    mine_t = d // apart

    @pl.when(owner)
    def _():
        wait_bytes(u_t.at[pl.ds(0, nseq - 1)], u_recv.at[1])
        u_a[mine_t] = total_of(u_t, nseq).astype(BF)

        def step(i, carry):
            copy_start(
                u_a.at[mine_t],
                u_a.at[mine_t],
                u_send.at[KV + 1],
                u_recv.at[2],
                (dp_peer(i), s),
            )
            return carry

        lax.fori_loop(1, ndp, step, 0)

    wait_bytes(g_t.at[pl.ds(0, nseq - 1)], ar_recv.at[1])
    g_a[d] = total_of(g_t, nseq).astype(BF)
    spread(lambda p: g_a.at[d], g_a, 2)

    @pl.when(owner)
    def _():
        wait_bytes(u_a.at[pl.ds(0, KV - 1)], u_recv.at[2])

    @pl.when(jnp.logical_not(owner))
    def _():
        wait_bytes(u_a, u_recv.at[2])

    for t in range(KV):
        upg_ref[:, t * HEAD : (t + 1) * HEAD] = u_a[t].astype(F32)
    wait_bytes(g_a.at[pl.ds(0, ndp - 1)], ar_recv.at[2])
    for t in range(ndp):
        gdown_ref[:, t * n_share : (t + 1) * n_share] = g_a[t].astype(F32)

    for kind, buf in enumerate((sa0, sb0, sa1, sb1, sret)):
        wait_sent(buf, dp_send.at[kind])
    wait_sent(sb2, dp_send.at[7])
    att_copy.wait()
    wait_sent(srg, dp_send.at[5], per_peer)
    wait_sent(sx, dp_send.at[6], per_peer)
    for piece, buf in enumerate((wa, wb)):
        for hop in range(1, hops + 1):
            ring(piece, buf, hop).wait_send()
        for hop in range(hops + 1):
            sibling(piece, buf, hop).wait_send()
    for w in range(back):
        rg_copy(w).wait_send()
    wait_bytes(g_s.at[pl.ds(0, ndp - 1)], ar_send.at[0])
    wait_bytes(g_t.at[pl.ds(0, nseq - 1)], ar_send.at[1])
    wait_bytes(g_a.at[pl.ds(0, ndp - 1)], ar_send.at[2])
    for t in range(KV):

        @pl.when(d != t * apart)
        def _():
            wait_bytes(u_s.at[t], u_send.at[t])

    @pl.when(owner)
    def _():
        wait_bytes(u_t.at[pl.ds(0, nseq - 1)], u_send.at[KV])
        wait_bytes(u_r.at[pl.ds(0, ndp - 1)], u_send.at[KV + 1])


def hand_over(a, b, c, a_out, b_out, c_out):
    a_out[...] = a[...]
    b_out[...] = b[...]
    c_out[...] = c[...]


def shards(nx, hops, hidden, q, k, v, up, group, slot, labels, down, upw):
    ndp = lax.axis_size("dp")
    nseq = lax.axis_size("seq")
    tok = hidden.shape[0]
    slots = 4 * tok
    back = 2 * hops
    lines = 2 * tok // SPAN
    share = hidden.shape[1] // ndp
    dma = pltpu.SemaphoreType.DMA
    widths = (2 * HEAD, 2 * HEAD, 5 * HEAD, 2 * HEAD, 2 * HEAD)
    scratch = (
        [pltpu.VMEM((slots, n), BF) for n in widths]
        + [pltpu.VMEM((slots, n), BF) for n in widths]
        + [
            pltpu.VMEM(((back + 2) * tok, 5 * HEAD), BF),
            pltpu.VMEM(((back + 2) * tok, 4 * HEAD), BF),
            pltpu.VMEM((2, RATIO * tok, (back + 1) * tok), BF),
            pltpu.VMEM((tok, (back + 1) * tok), F32),
            pltpu.VMEM((2 * tok, HEAD), BF),
        ]
        + [pltpu.VMEM((slots, HEAD), BF)] * 2
        + [pltpu.VMEM((lines, 2, HEAD), F32)] * 2
        + [pltpu.VMEM((lines, 1, HEAD), F32)] * 2
        + [pltpu.VMEM((back * RANK, tok), BF)] * 2
        + [
            pltpu.VMEM((ndp, RANK, share), BF),
            pltpu.VMEM((ndp, RANK, share), BF),
            pltpu.VMEM((nseq, RANK, share), BF),
            pltpu.VMEM((ndp, RANK, share), BF),
            pltpu.VMEM((KV, RANK, HEAD), BF),
            pltpu.VMEM((ndp, RANK, HEAD), BF),
            pltpu.VMEM((nseq, RANK, HEAD), BF),
            pltpu.VMEM((KV, RANK, HEAD), BF),
            dma((8,)),
            dma((8,)),
            dma((2, hops + 1)),
            dma((2, hops + 1)),
            dma((2, hops + 1)),
            dma((2, hops + 1)),
            dma((back,)),
            dma((back,)),
            dma((3,)),
            dma((3,)),
            dma((KV + 2,)),
            dma((3,)),
            pltpu.VMEM((2 * tok, tok), BF),
            pltpu.VMEM((2 * tok, tok), BF),
            pltpu.VMEM((slots, 2 * tok), BF),
            pltpu.VMEM((slots, 2 * tok), BF),
            pltpu.VMEM((2 * tok, slots), BF),
            pltpu.VMEM((tok, KV * HEAD), BF),
        ]
        + [pltpu.VMEM(a.shape, BF) for a in (hidden, q, k, v, up, q)]
        + [dma((6,))]
    )
    vmem = pl.BlockSpec(memory_space=pltpu.VMEM)
    anywhere = pl.BlockSpec(memory_space=pl.ANY)
    results = pl.pallas_call(
        functools.partial(kernel, ndp, nx, nseq, hops),
        out_shape=(
            jax.ShapeDtypeStruct(q.shape, BF),
            jax.ShapeDtypeStruct(down.shape, F32),
            jax.ShapeDtypeStruct(upw.shape, F32),
        ),
        in_specs=[anywhere] * 5 + [vmem] * 5,
        out_specs=(anywhere, vmem, vmem),
        scratch_shapes=scratch,
        compiler_params=pltpu.CompilerParams(
            collective_id=0, has_side_effects=True, vmem_limit_bytes=56 * 1024 * 1024
        ),
        cost_estimate=pl.CostEstimate(
            flops=4 * 10**9, bytes_accessed=4 * 10**6, transcendentals=2400000
        ),
    )(
        hidden,
        q,
        k,
        v,
        up,
        group.reshape(1, tok),
        slot.reshape(1, tok),
        labels,
        down,
        upw,
    )
    return pl.pallas_call(
        hand_over,
        out_shape=tuple(jax.ShapeDtypeStruct(a.shape, a.dtype) for a in results),
        in_specs=[vmem] * 3,
        out_specs=(vmem,) * 3,
        cost_estimate=pl.CostEstimate(flops=0, bytes_accessed=1600000, transcendentals=0),
    )(*results)


def build(mesh, nx, hops):
    rows = P(("dp", "seq"), None)
    return jax.shard_map(
        functools.partial(shards, nx, hops),
        mesh=mesh,
        in_specs=(
            rows,
            rows,
            rows,
            rows,
            rows,
            P(("dp", "seq")),
            P(("dp", "seq")),
            P("dp", "seq"),
            P(),
            P(),
        ),
        out_specs=(rows, P(), P()),
        check_vma=False,
    )


def solution(mesh):
    return build(mesh, 4, 4)
```

time: 120 us -> 101 us (0.84)
  Pallas kernels: 116 us -> 101 us
  local copies, waits for them, and re-layouts: 3.3 us -> 0 us
    pallas_call x1, Pallas kernels: 116 us -> 98.5 us  [shards(): pl.pallas_call(functools.partial(kernel, ndp, nx, nseq, hops), out_shape=...]
    unnamed x7 -> x0, local copies, waits for them, and re-layouts: 3.3 us -> none
    pallas_call x0 -> x1, Pallas kernels: none -> 2.03 us  [shards(): pl.pallas_call(hand_over, out_shape=tuple((jax.ShapeDtypeStruct(a.shape,...]
where the time goes in v2:
time: 101 us
  Pallas kernels  101 us (100%)
    pallas_call x1, Pallas kernels, shards(): pl.pallas_call(functools.partial(kernel, ndp, nx, nseq, hops), out_shape=...  98.5 us
    pallas_call x1, Pallas kernels, shards(): pl.pallas_call(hand_over, out_shape=tuple((jax.ShapeDtypeStruct(a.shape,...  2.03 us

profile of v2, /device:TPU:1, one launch (start us, length us, event | category | flops | bytes accessed | tf_op | source)
XLA Modules:
  0.0 101.1 jit_solution(6767563766926391715)
XLA Ops:
  0.6 98.5 %shard_map.121 = (bf16[128,2048]{1,0:T(8,128)(2,1)}, f32[16,4096]{1,0:T(8,128)}, f32[16,512]{1,0:T(8,128)}) custom-call(bf16[128,4096]{1,0:T(8,128)(2,1)} %hidden_in.1, bf16[128,2048]{1,0:T(8,128)(2,1)} %q_in.1, bf16[128,512]{1,0:T(8,128)(2,1)} %k_in.1, bf16[128,512]{1,0:T(8,128)(2,1)} %v_in.1, bf16[128,2048]{1,0:T(8,128)(2,1)} %up_in.1, s32[1,128]{1,0:T(1,128)} %bitcast.2, ...), custom_call_target="tpu_custom_call" | custom-call | flops 4000000000 | bytes 4000000 | tf_op jit(solution)/shard_map/pallas_call | solution.py:654
  99.1 2.0 %shard_map.122 = (bf16[128,2048]{1,0:T(8,128)(2,1)}, f32[16,4096]{1,0:T(8,128)}, f32[16,512]{1,0:T(8,128)}) custom-call(bf16[128,2048]{1,0:T(8,128)(2,1)} %get-tuple-element.6.a, f32[16,4096]{1,0:T(8,128)} %get-tuple-element.7.b, f32[16,512]{1,0:T(8,128)} %get-tuple-element.8.c), custom_call_target="tpu_custom_call" | custom-call | bytes 1600000 | tf_op jit(solution)/shard_map/pallas_call | solution.py:682

commit v3 on v2

--- a/solution.py
+++ b/solution.py
@@ -16,7 +16,6 @@
 KV = 4
 RATIO = 4
 ONE_LANE = 16
-DOC_LANE = 17
 SPAN = HEAD // RANK
 
 
@@ -54,18 +53,25 @@
     att_out,
     gdown_ref,
     upg_ref,
-    sa0,
-    sb0,
+    sk0,
+    sv0,
+    sk1,
+    sv1,
     sa1,
     sb1,
     sb2,
-    ra0,
-    rb0,
+    rk0,
+    rv0,
+    rk1,
+    rv1,
     ra1,
     rb1,
     rb2,
-    wa,
-    wb,
+    wk0,
+    wv0,
+    wk1,
+    wv1,
+    wx,
     pbuf,
     bias,
     aret,
@@ -138,14 +144,17 @@
     s = lax.axis_index("seq")
     z, x = d // nx, d % nx
     y, c = s // 2, s % 2
-    stride = 13 if ndp == 32 else 1
+
+    def far_first(i, n):
+        return (n + n // 2 + ((i + 1) // 2) * (2 * ((i + 1) % 2) - 1)) % n
 
     def dp_peer(step):
-        off = (step * stride) % ndp
-        return ((z + off // nx) % nz) * nx + (x + off % nx) % nx
+        i = step - 1
+        return ((z + far_first(i // nx, nz)) % nz) * nx + (x + far_first(i % nx, nx)) % nx
 
     def seq_peer(step):
-        return (s + step) % nseq
+        i = step - 1
+        return ((y + far_first(i // 2, ny)) % ny) * 2 + (c + 1 - i % 2) % 2
 
     barrier = pltpu.get_barrier_semaphore()
 
@@ -233,31 +242,20 @@
         return rows[:, cc * HEAD : (cc + 1) * HEAD]
 
     loads[1].wait()
-    keys = k_ref[...]
-    xa0 = jnp.concatenate(
-        [
-            jnp.concatenate([kv_cols(keys, 2 * f), kv_cols(value, 2 * f)], axis=1)
-            for f in range(2)
-        ],
-        axis=0,
-    )
-    sa0[...] = mm(pack[...], xa0).astype(BF)
-
+
+    def both_halves(ref, first):
+        return jnp.concatenate([kv_cols(ref[...], 2 * f + first) for f in range(2)], axis=0)
+
+    sk0[...] = mm(pack[...], both_halves(k_ref, 0)).astype(BF)
     pl.semaphore_wait(barrier, ndp + nseq - 2)
+    send_dp(sk0, rk0, 0)
     send_dp(sx, rx, 6, per_peer)
-    send_dp(sa0, ra0, 0)
-
-    keys = k_ref[...]
-    value = value_ref[...]
-    xb0 = jnp.concatenate(
-        [
-            jnp.concatenate([kv_cols(keys, 2 * f + 1), kv_cols(value, 2 * f + 1)], axis=1)
-            for f in range(2)
-        ],
-        axis=0,
-    )
-    sb0[...] = mm(pack[...], xb0).astype(BF)
-    send_dp(sb0, rb0, 1)
+    sv0[...] = mm(pack[...], both_halves(value_ref, 0)).astype(BF)
+    send_dp(sv0, rv0, 1)
+    sk1[...] = mm(pack[...], both_halves(k_ref, 1)).astype(BF)
+    send_dp(sk1, rk1, 8)
+    sv1[...] = mm(pack[...], both_halves(value_ref, 1)).astype(BF)
+    send_dp(sv1, rv1, 9)
 
     half_heads = KV * RATIO // 2
     half_width = half_heads * HEAD
@@ -288,13 +286,13 @@
     sb2[...] = mm(pack[...], xb1[:, quad // 2 :]).astype(BF)
     send_dp(sb2, rb2, 7)
 
-    def place_of(hop, core):
-        return rows_of((hops - hop) * 2 + core, tok)
+    def place_of(hop, core, buf):
+        return rows_of((hops - hop) * 2 + core, buf.shape[0] // (back + 2))
 
     def ring(piece, buf, hop):
         return pltpu.make_async_remote_copy(
-            src_ref=buf.at[place_of(hop - 1, c)],
-            dst_ref=buf.at[place_of(hop, c)],
+            src_ref=buf.at[place_of(hop - 1, c, buf)],
+            dst_ref=buf.at[place_of(hop, c, buf)],
             send_sem=ring_send.at[piece, hop],
             recv_sem=ring_recv.at[piece, hop],
             device_id=(d, ((y + 1) % ny) * 2 + c),
@@ -303,8 +301,8 @@
 
     def sibling(piece, buf, hop):
         return pltpu.make_async_remote_copy(
-            src_ref=buf.at[place_of(hop, c)],
-            dst_ref=buf.at[place_of(hop, c)],
+            src_ref=buf.at[place_of(hop, c, buf)],
+            dst_ref=buf.at[place_of(hop, c, buf)],
             send_sem=sib_send.at[piece, hop],
             recv_sem=sib_recv.at[piece, hop],
             device_id=(d, y * 2 + 1 - c),
@@ -312,7 +310,7 @@
         )
 
     def sibling_arrived(piece, buf, hop):
-        wait_bytes(buf.at[place_of(hop, 1 - c)], sib_recv.at[piece, hop])
+        wait_bytes(buf.at[place_of(hop, 1 - c, buf)], sib_recv.at[piece, hop])
 
     wait_bytes(rx, dp_recv.at[6])
     slot_in = jnp.max(from_lines(rx[:, 1:2, :]), axis=1, keepdims=True)
@@ -326,23 +324,33 @@
         unpack[:, f * tok : (f + 1) * tok] = chosen.astype(BF)
         unpack_t[f * tok : (f + 1) * tok, :] = chosen.T.astype(BF)
     reduced_in = t_mm(unsmall[...], from_lines(rx[:, 0:1, :]).astype(BF)).astype(BF)
-    own_tile = mm(reduced_in, fold)
-    wait_bytes(ra0, dp_recv.at[0])
-    arranged = mm(unpack_t[...], ra0[...]).astype(BF)
-    doc_col = jnp.broadcast_to(label_ref[...].astype(F32), (tok, tok)).T
-    doc = lane.astype(F32) == doc_col + float(DOC_LANE)
-    own_tile = jnp.where((lane == ONE_LANE) | doc, 1.0, own_tile).astype(BF)
-    own = place_of(0, c)
-    wa[own, :] = jnp.concatenate(
-        [arranged[:tok, :], arranged[tok:, :], own_tile], axis=1
-    )
-    ring(0, wa, 1).start()
-    sibling(0, wa, 0).start()
-    wait_bytes(rb0, dp_recv.at[1])
-    arranged = mm(unpack_t[...], rb0[...]).astype(BF)
-    wb[own, :] = jnp.concatenate([arranged[:tok, :], arranged[tok:, :]], axis=1)
-    ring(1, wb, 1).start()
-    sibling(1, wb, 0).start()
+    fold_all = jnp.where(sub % RANK == lane % RANK, 1.0, 0.0).astype(BF)
+    reduced_in = jnp.where(lane // RANK == sub % SPAN, mm(reduced_in, fold_all), 0.0)
+    thin = tok // SPAN
+    reduced_in = jnp.sum(reduced_in.reshape(thin, SPAN, HEAD), axis=1)
+    doc_row = jnp.broadcast_to(label_ref[...].astype(F32), (thin, tok))
+    wx[place_of(0, c, wx), :] = jnp.concatenate([reduced_in, doc_row], axis=0).astype(BF)
+    pieces = ((0, wk0), (1, wx), (2, wv0), (3, wk1), (4, wv1))
+
+    def set_out(piece, buf):
+        ring(piece, buf, 1).start()
+        sibling(piece, buf, 0).start()
+
+    for piece, buf, arrived, kind in (
+        (0, wk0, rk0, 0),
+        (2, wv0, rv0, 1),
+        (3, wk1, rk1, 8),
+        (4, wv1, rv1, 9),
+    ):
+        wait_bytes(arrived, dp_recv.at[kind])
+        arranged = mm(unpack_t[...], arrived[...]).astype(BF)
+        buf[place_of(0, c, buf), :] = jnp.concatenate(
+            [arranged[:tok, :], arranged[tok:, :]], axis=1
+        )
+        set_out(piece, buf)
+        if piece == 0:
+            set_out(1, wx)
+
     def pass_on(piece, buf, hop):
         ring(piece, buf, hop).wait_recv()
         if hop < hops:
@@ -350,19 +358,28 @@
         sibling(piece, buf, hop).start()
 
     for hop in range(1, hops):
-        pass_on(0, wa, hop)
-        pass_on(1, wb, hop)
+        for piece, buf in pieces:
+            pass_on(piece, buf, hop)
     wait_bytes(ra1, dp_recv.at[2])
     queries = mm(unpack_t[...], ra1[...]).astype(BF)
-    pass_on(0, wa, hops)
+    for piece, buf in pieces[:3]:
+        pass_on(piece, buf, hops)
     for hop in range(hops + 1):
-        sibling_arrived(0, wa, hop)
-
-    window = rows_of(c, tok)
-    window = pl.ds(window.start, win)
-    tiles = wa[window, 4 * HEAD :]
-    doc_q = jnp.where(doc, 1.0, 0.0).astype(BF)
-    together = mm_t(doc_q, tiles) > 0.5
+        for piece, buf in pieces[:3]:
+            sibling_arrived(piece, buf, hop)
+
+    window = pl.ds(pl.multiple_of(c * tok, tok), win)
+    thin_win = pl.ds(pl.multiple_of(c * 2 * thin, 2 * thin), (back + 1) * 2 * thin)
+    thin_rows = wx[thin_win, :].astype(F32).reshape(back + 1, 2 * thin, HEAD)
+    doc_keys = jnp.concatenate([thin_rows[w, thin : thin + 1] for w in range(back + 1)], axis=1)
+    doc_col = jnp.broadcast_to(label_ref[...].astype(F32), (tok, tok)).T
+    together = doc_col[:, 0:1] == doc_keys
+    n_thin = (back + 1) * thin
+    tiles = thin_rows[:, :thin].reshape(n_thin, 1, HEAD)
+    tiles = jnp.broadcast_to(tiles, (n_thin, SPAN, HEAD)).reshape(win, HEAD)
+    win_lane = iota((win, HEAD), 1)
+    tiles = jnp.where(win_lane // RANK == iota((win, HEAD), 0) % SPAN, tiles, 0.0).astype(BF)
+    tiles = jnp.where(win_lane == ONE_LANE, 1.0, mm(tiles, fold)).astype(BF)
     col = iota((tok, win), 1)
     seen = together & (col - back * tok <= iota((tok, win), 0)) & (col >= (back - s) * tok)
     bias[...] = jnp.where(seen, 0.0, -1e30)
@@ -371,12 +388,10 @@
     narrow_in = [queries[f * tok : (f + 1) * tok, quad:].astype(F32) for f in range(2)]
     returned = [jnp.zeros((tok, HEAD), F32) for _ in range(2)]
 
-    def attend(piece, buf, arranged, f, first, count):
+    def attend(piece, wk, wv, arranged, f, first, count):
         cc = 2 * f + piece
-        key = buf[window, 2 * f * HEAD : (2 * f + 1) * HEAD]
-        val = jnp.concatenate(
-            [buf[window, (2 * f + 1) * HEAD : (2 * f + 2) * HEAD], tiles], axis=1
-        )
+        key = wk[window, f * HEAD : (f + 1) * HEAD]
+        val = jnp.concatenate([wv[window, f * HEAD : (f + 1) * HEAD], tiles], axis=1)
         query = jnp.concatenate(
             [
                 arranged[f * tok : (f + 1) * tok, h * HEAD : (h + 1) * HEAD]
@@ -408,16 +423,18 @@
         return t_mm(jnp.concatenate(lefts, axis=0), weights)
 
     half = RATIO // 2
-    rg_total = attend(0, wa, queries, 0, 0, RATIO)
-    pass_on(1, wb, hops)
-    rg_total = rg_total + attend(0, wa, queries, 1, 0, RATIO)
+    rg_total = attend(0, wk0, wv0, queries, 0, 0, RATIO)
+    for piece, buf in pieces[3:]:
+        pass_on(piece, buf, hops)
+    rg_total = rg_total + attend(0, wk0, wv0, queries, 1, 0, RATIO)
     for hop in range(hops + 1):
-        sibling_arrived(1, wb, hop)
+        for piece, buf in pieces[3:]:
+            sibling_arrived(piece, buf, hop)
     for arrived, kind, first in ((rb1, 3, 0), (rb2, 7, half)):
         wait_bytes(arrived, dp_recv.at[kind])
         queries = mm(unpack_t[...], arrived[...]).astype(BF)
         for f in range(2):
-            rg_total = rg_total + attend(1, wb, queries, f, first, half)
+            rg_total = rg_total + attend(1, wk1, wv1, queries, f, first, half)
     att_copy.start()
 
     def rg_copy(w):
@@ -560,13 +577,21 @@
     for t in range(ndp):
         gdown_ref[:, t * n_share : (t + 1) * n_share] = g_a[t].astype(F32)
 
-    for kind, buf in enumerate((sa0, sb0, sa1, sb1, sret)):
+    for kind, buf in (
+        (0, sk0),
+        (1, sv0),
+        (8, sk1),
+        (9, sv1),
+        (2, sa1),
+        (3, sb1),
+        (7, sb2),
+        (4, sret),
+    ):
         wait_sent(buf, dp_send.at[kind])
-    wait_sent(sb2, dp_send.at[7])
     att_copy.wait()
     wait_sent(srg, dp_send.at[5], per_peer)
     wait_sent(sx, dp_send.at[6], per_peer)
-    for piece, buf in enumerate((wa, wb)):
+    for piece, buf in pieces:
         for hop in range(1, hops + 1):
             ring(piece, buf, hop).wait_send()
         for hop in range(hops + 1):
@@ -603,13 +628,16 @@
     lines = 2 * tok // SPAN
     share = hidden.shape[1] // ndp
     dma = pltpu.SemaphoreType.DMA
-    widths = (2 * HEAD, 2 * HEAD, 5 * HEAD, 2 * HEAD, 2 * HEAD)
+    widths = (HEAD, HEAD, HEAD, HEAD, 5 * HEAD, 2 * HEAD, 2 * HEAD)
     scratch = (
         [pltpu.VMEM((slots, n), BF) for n in widths]
         + [pltpu.VMEM((slots, n), BF) for n in widths]
         + [
-            pltpu.VMEM(((back + 2) * tok, 5 * HEAD), BF),
-            pltpu.VMEM(((back + 2) * tok, 4 * HEAD), BF),
+            pltpu.VMEM(((back + 2) * tok, 2 * HEAD), BF),
+            pltpu.VMEM(((back + 2) * tok, 2 * HEAD), BF),
+            pltpu.VMEM(((back + 2) * tok, 2 * HEAD), BF),
+            pltpu.VMEM(((back + 2) * tok, 2 * HEAD), BF),
+            pltpu.VMEM(((back + 2) * 2 * (tok // SPAN), HEAD), BF),
             pltpu.VMEM((2, RATIO * tok, (back + 1) * tok), BF),
             pltpu.VMEM((tok, (back + 1) * tok), F32),
             pltpu.VMEM((2 * tok, HEAD), BF),
@@ -627,12 +655,12 @@
             pltpu.VMEM((ndp, RANK, HEAD), BF),
             pltpu.VMEM((nseq, RANK, HEAD), BF),
             pltpu.VMEM((KV, RANK, HEAD), BF),
-            dma((8,)),
-            dma((8,)),
-            dma((2, hops + 1)),
-            dma((2, hops + 1)),
-            dma((2, hops + 1)),
-            dma((2, hops + 1)),
+            dma((10,)),
+            dma((10,)),
+            dma((5, hops + 1)),
+            dma((5, hops + 1)),
+            dma((5, hops + 1)),
+            dma((5, hops + 1)),
             dma((back,)),
             dma((back,)),
             dma((3,)),

time: 101 us -> 97.6 us (0.966)
  Pallas kernels: 101 us -> 96.6 us
    pallas_call x1, Pallas kernels: 98.5 us -> 94.6 us  [shards(): pl.pallas_call(functools.partial(kernel, ndp, nx, nseq, hops), out_shape=...]
where the time goes in v3:
time: 97.6 us; the launch traced here: 97.2 us
  Pallas kernels  96.6 us (99%)
    pallas_call x1, Pallas kernels, shards(): pl.pallas_call(functools.partial(kernel, ndp, nx, nseq, hops), out_shape=...  94.6 us
    pallas_call x1, Pallas kernels, shards(): pl.pallas_call(hand_over, out_shape=tuple((jax.ShapeDtypeStruct(a.shape,...  2.03 us

profile of v3, /device:TPU:1, one launch (start us, length us, event | category | flops | bytes accessed | tf_op | source)
XLA Modules:
  0.0 97.2 jit_solution(7740260981900953759)
XLA Ops:
  0.6 94.6 %shard_map.121 = (bf16[128,2048]{1,0:T(8,128)(2,1)}, f32[16,4096]{1,0:T(8,128)}, f32[16,512]{1,0:T(8,128)}) custom-call(bf16[128,4096]{1,0:T(8,128)(2,1)} %hidden_in.1, bf16[128,2048]{1,0:T(8,128)(2,1)} %q_in.1, bf16[128,512]{1,0:T(8,128)(2,1)} %k_in.1, bf16[128,512]{1,0:T(8,128)(2,1)} %v_in.1, bf16[128,2048]{1,0:T(8,128)(2,1)} %up_in.1, s32[1,128]{1,0:T(1,128)} %bitcast.2, ...), custom_call_target="tpu_custom_call" | custom-call | flops 4000000000 | bytes 4000000 | tf_op jit(solution)/shard_map/pallas_call | solution.py:682
  95.2 2.0 %shard_map.122 = (bf16[128,2048]{1,0:T(8,128)(2,1)}, f32[16,4096]{1,0:T(8,128)}, f32[16,512]{1,0:T(8,128)}) custom-call(bf16[128,2048]{1,0:T(8,128)(2,1)} %get-tuple-element.6.a, f32[16,4096]{1,0:T(8,128)} %get-tuple-element.7.b, f32[16,512]{1,0:T(8,128)} %get-tuple-element.8.c), custom_call_target="tpu_custom_call" | custom-call | bytes 1600000 | tf_op jit(solution)/shard_map/pallas_call | solution.py:710

commit v4 on v3

--- a/solution.py
+++ b/solution.py
@@ -59,14 +59,12 @@
     sv1,
     sa1,
     sb1,
-    sb2,
     rk0,
     rv0,
     rk1,
     rv1,
     ra1,
     rb1,
-    rb2,
     wk0,
     wv0,
     wk1,
@@ -281,10 +279,8 @@
     sa1[...] = mm(pack[...], xa1).astype(BF)
     send_dp(sa1, ra1, 2)
     xb1 = jnp.concatenate([q_cols(2 * f + 1) for f in range(2)], axis=0)
-    sb1[...] = mm(pack[...], xb1[:, : quad // 2]).astype(BF)
+    sb1[...] = mm(pack[...], xb1).astype(BF)
     send_dp(sb1, rb1, 3)
-    sb2[...] = mm(pack[...], xb1[:, quad // 2 :]).astype(BF)
-    send_dp(sb2, rb2, 7)
 
     def place_of(hop, core, buf):
         return rows_of((hops - hop) * 2 + core, buf.shape[0] // (back + 2))
@@ -422,7 +418,6 @@
             lefts.append((left[:, :RANK] * inv[rows]).astype(BF))
         return t_mm(jnp.concatenate(lefts, axis=0), weights)
 
-    half = RATIO // 2
     rg_total = attend(0, wk0, wv0, queries, 0, 0, RATIO)
     for piece, buf in pieces[3:]:
         pass_on(piece, buf, hops)
@@ -430,11 +425,10 @@
     for hop in range(hops + 1):
         for piece, buf in pieces[3:]:
             sibling_arrived(piece, buf, hop)
-    for arrived, kind, first in ((rb1, 3, 0), (rb2, 7, half)):
-        wait_bytes(arrived, dp_recv.at[kind])
-        queries = mm(unpack_t[...], arrived[...]).astype(BF)
-        for f in range(2):
-            rg_total = rg_total + attend(1, wk1, wv1, queries, f, first, half)
+    wait_bytes(rb1, dp_recv.at[3])
+    queries = mm(unpack_t[...], rb1[...]).astype(BF)
+    for f in range(2):
+        rg_total = rg_total + attend(1, wk1, wv1, queries, f, 0, RATIO)
     att_copy.start()
 
     def rg_copy(w):
@@ -571,11 +565,9 @@
     def _():
         wait_bytes(u_a, u_recv.at[2])
 
-    for t in range(KV):
-        upg_ref[:, t * HEAD : (t + 1) * HEAD] = u_a[t].astype(F32)
+    upg_ref[...] = u_a[...]
     wait_bytes(g_a.at[pl.ds(0, ndp - 1)], ar_recv.at[2])
-    for t in range(ndp):
-        gdown_ref[:, t * n_share : (t + 1) * n_share] = g_a[t].astype(F32)
+    gdown_ref[...] = g_a[...]
 
     for kind, buf in (
         (0, sk0),
@@ -584,7 +576,6 @@
         (9, sv1),
         (2, sa1),
         (3, sb1),
-        (7, sb2),
         (4, sret),
     ):
         wait_sent(buf, dp_send.at[kind])
@@ -613,10 +604,12 @@
         wait_bytes(u_r.at[pl.ds(0, ndp - 1)], u_send.at[KV + 1])
 
 
-def hand_over(a, b, c, a_out, b_out, c_out):
-    a_out[...] = a[...]
-    b_out[...] = b[...]
-    c_out[...] = c[...]
+def hand_over(att, down, up, att_out, down_out, up_out):
+    att_out[...] = att[...]
+    for part, out in ((down, down_out), (up, up_out)):
+        width = part.shape[2]
+        for t in range(part.shape[0]):
+            out[:, t * width : (t + 1) * width] = part[t].astype(F32)
 
 
 def shards(nx, hops, hidden, q, k, v, up, group, slot, labels, down, upw):
@@ -628,7 +621,7 @@
     lines = 2 * tok // SPAN
     share = hidden.shape[1] // ndp
     dma = pltpu.SemaphoreType.DMA
-    widths = (HEAD, HEAD, HEAD, HEAD, 5 * HEAD, 2 * HEAD, 2 * HEAD)
+    widths = (HEAD, HEAD, HEAD, HEAD, 5 * HEAD, 4 * HEAD)
     scratch = (
         [pltpu.VMEM((slots, n), BF) for n in widths]
         + [pltpu.VMEM((slots, n), BF) for n in widths]
@@ -683,8 +676,8 @@
         functools.partial(kernel, ndp, nx, nseq, hops),
         out_shape=(
             jax.ShapeDtypeStruct(q.shape, BF),
-            jax.ShapeDtypeStruct(down.shape, F32),
-            jax.ShapeDtypeStruct(upw.shape, F32),
+            jax.ShapeDtypeStruct((ndp, RANK, share), BF),
+            jax.ShapeDtypeStruct((KV, RANK, HEAD), BF),
         ),
         in_specs=[anywhere] * 5 + [vmem] * 5,
         out_specs=(anywhere, vmem, vmem),
@@ -709,7 +702,11 @@
     )
     return pl.pallas_call(
         hand_over,
-        out_shape=tuple(jax.ShapeDtypeStruct(a.shape, a.dtype) for a in results),
+        out_shape=(
+            jax.ShapeDtypeStruct(q.shape, BF),
+            jax.ShapeDtypeStruct(down.shape, F32),
+            jax.ShapeDtypeStruct(upw.shape, F32),
+        ),
         in_specs=[vmem] * 3,
         out_specs=(vmem,) * 3,
         cost_estimate=pl.CostEstimate(flops=0, bytes_accessed=1600000, transcendentals=0),

time: 97.6 us -> 96.9 us (level)
  no operation moved by 1% of the time
where the time goes in v4:
time: 96.9 us; the launch traced here: 96.8 us
  Pallas kernels  96.1 us (99%)
    pallas_call x1, Pallas kernels, shards(): pl.pallas_call(functools.partial(kernel, ndp, nx, nseq, hops), out_shape=...  94.1 us
    pallas_call x1, Pallas kernels, shards(): pl.pallas_call(hand_over, out_shape=(jax.ShapeDtypeStruct(q.shape, BF), j...  2.02 us

profile of v4, /device:TPU:1, one launch (start us, length us, event | category | flops | bytes accessed | tf_op | source)
XLA Modules:
  0.0 96.8 jit_solution(13789031546376483799)
XLA Ops:
  0.6 94.1 %shard_map.121 = (bf16[128,2048]{1,0:T(8,128)(2,1)}, bf16[32,16,128]{2,1,0:T(8,128)(2,1)}, bf16[4,16,128]{2,1,0:T(8,128)(2,1)}) custom-call(bf16[128,4096]{1,0:T(8,128)(2,1)} %hidden_in.1, bf16[128,2048]{1,0:T(8,128)(2,1)} %q_in.1, bf16[128,512]{1,0:T(8,128)(2,1)} %k_in.1, bf16[128,512]{1,0:T(8,128)(2,1)} %v_in.1, bf16[128,2048]{1,0:T(8,128)(2,1)} %up_in.1, ...), custom_call_target="tpu_custom_call" | custom-call | flops 4000000000 | bytes 4000000 | tf_op jit(solution)/shard_map/pallas_call | solution.py:675
  94.8 2.0 %shard_map.122 = (bf16[128,2048]{1,0:T(8,128)(2,1)}, f32[16,4096]{1,0:T(8,128)}, f32[16,512]{1,0:T(8,128)}) custom-call(bf16[128,2048]{1,0:T(8,128)(2,1)} %get-tuple-element.6.att, bf16[32,16,128]{2,1,0:T(8,128)(2,1)} %get-tuple-element.7.down, bf16[4,16,128]{2,1,0:T(8,128)(2,1)} %get-tuple-element.8.up), custom_call_target="tpu_custom_call" | custom-call | bytes 1600000 | tf_op jit(solution)/shard_map/pallas_call | solution.py:703
